TPU v7x, 1024 devices: a whole 4x4x32 slice. The times are simulated.
1024 devices in a mesh: comp: 2 (over core), gy: 8 (over y, x_hi), gx: 64 (over x_lo, z).
Axes of the slice: x: 4 (x_hi: 2, x_lo: 2; x = x_hi * 2 + x_lo), y: 4, z: 32, core: 2. Of those that a mesh axis runs over, the one named last changes fastest.
Arguments:
- ocean_state: float32 [16, 8, 256, 1024], P('comp', None, 'gx', 'gy'), may hold values from -4 to 4, as said below
- irradiance: float32 [256, 1024], P('gx', 'gy'), may hold values from 0.5 to 4
- land_mask: int32 [256, 1024], P('gx', 'gy'), may hold values 0 or 1
- bottom_level: int32 [256, 1024], P('gx', 'gy'), may hold values from 1 to 8
Outputs:
- new_state: float32 [16, 8, 256, 1024], P('comp', None, 'gx', 'gy')
Inputs may be any that keep to these rules, and one draw needn't show every extreme that they name: `ocean_state`: channels 0 to 3 hold velocity along x, velocity along y, temperature and salinity now, channels 4 to 7 the same one step earlier; the 8 tracer channels are positive.
All inputs are finite; a program needn't handle non-finite values. No bound on the sum of `land_mask` on one device may be relied on, other than what follows from the above.
Results may differ from a plain program's by a relative error of at most 0.0003.
Values sent between devices are 32-bit elements; how exact they have to be, the bound alone decides.
A program may use at most 32 MiB of HBM per device.

v0:
```python
import jax
import jax.numpy as jnp
from jax import lax
from jax.sharding import PartitionSpec as P

STEPS = 2


TIME_STEP = 0.1
VISCOSITY = 0.2
DIFFUSION = 0.2
ASSELIN_GAIN = 0.1
THERMAL_EXPAND = 0.2
HALINE_CONTRACT = 0.8
GRAVITY_STEP = 0.1
CORIOLIS_BASE = 0.3
CORIOLIS_SLOPE = 0.4
MIXING_FLOOR = 0.05
MIXING_SPAN = 1.0
STRATIFICATION = 4.0
HEATING_GAIN = 3.0
WATER_ABSORB = 0.08
PIGMENT_ABSORB = 0.05
LIGHT_HALF = 0.5
THERMAL_GAIN_PER = 0.06
GROWTH_SMALL = 0.6
GROWTH_LARGE = 0.9
NUTRIENT_HALF_SMALL = 0.2
NUTRIENT_HALF_LARGE = 0.8
GRAZING_RATE = 0.8
GRAZING_HALF = 1.0
PHYTO_DEATH = 0.1
ZOOPLANKTON_DEATH = 0.15
EXCRETION = 0.1
ASSIMILATION = 0.7
REMINERAL_SMALL = 0.3
REMINERAL_LARGE = 0.1
NITRIFICATION = 0.2
OXYGEN_YIELD = 1.3
OXYGEN_DEMAND = 1.0


def extended(shard, sides, width, wrap):
    for axis, dim in sides:
        count, length = (lax.axis_size(axis), shard.shape[dim])
        up = [(i, (i + 1) % count) for i in range(count if wrap else count - 1)]
        down = [(j, i) for i, j in up]
        last = lax.slice_in_dim(shard, length - width, length, axis=dim)
        leading = lax.slice_in_dim(shard, 0, width, axis=dim)
        before = lax.ppermute(last, axis, up)
        after = lax.ppermute(leading, axis, down)
        shard = jnp.concatenate([before, shard, after], axis=dim)
    return shard


def broadcast(shard, axis, root):
    mine = lax.axis_index(axis) == root
    return lax.psum(jnp.where(mine, shard, jnp.zeros_like(shard)), axis)


def interior(field_in):
    return field_in[..., 1:-1, 1:-1]


def neighbours(field_in):
    return (
        field_in[..., 2:, 1:-1],
        field_in[..., :-2, 1:-1],
        field_in[..., 1:-1, 2:],
        field_in[..., 1:-1, :-2],
    )


def laplacian(field_in, entire_ocean_indicator):
    centre = interior(field_in)
    total = jnp.zeros_like(centre)
    for other, wet_other in zip(neighbours(field_in), neighbours(entire_ocean_indicator)):
        total = total + wet_other * (other - centre)
    return total * interior(entire_ocean_indicator)


def advection(east_speed, north_speed, field_in, entire_ocean_indicator):
    centre = interior(field_in)
    wet_centre = interior(entire_ocean_indicator)
    east_centre = interior(east_speed)
    north_centre = interior(north_speed)
    field_near = neighbours(field_in)
    wet_near = neighbours(entire_ocean_indicator)
    east_near = neighbours(east_speed)
    north_near = neighbours(north_speed)
    flux_east = (
        0.25 * (east_centre + east_near[0]) * (centre + field_near[0]) * wet_centre * wet_near[0]
    )
    flux_west = (
        0.25 * (east_centre + east_near[1]) * (centre + field_near[1]) * wet_centre * wet_near[1]
    )
    flux_north = (
        0.25 * (north_centre + north_near[2]) * (centre + field_near[2]) * wet_centre * wet_near[2]
    )
    flux_south = (
        0.25 * (north_centre + north_near[3]) * (centre + field_near[3]) * wet_centre * wet_near[3]
    )
    return flux_east - flux_west + flux_north - flux_south


def pressure_force(pressure, entire_ocean_indicator):
    centre = interior(pressure)
    wet_centre = interior(entire_ocean_indicator)
    near = neighbours(pressure)
    wet_near = neighbours(entire_ocean_indicator)
    force_east = (
        0.5 * wet_centre * (wet_near[0] * (near[0] - centre) + wet_near[1] * (centre - near[1]))
    )
    force_north = (
        0.5 * wet_centre * (wet_near[2] * (near[2] - centre) + wet_near[3] * (centre - near[3]))
    )
    return (force_east, force_north)


def ocean_water_mass_per_volume(thermal_state_grid, salt_content_grid, entire_ocean_indicator):
    return (
        HALINE_CONTRACT * salt_content_grid - THERMAL_EXPAND * thermal_state_grid
    ) * entire_ocean_indicator


def make_flow(dynamics_full, entire_ocean_indicator):
    density = ocean_water_mass_per_volume(
        dynamics_full[2], dynamics_full[3], entire_ocean_indicator
    )
    below = jnp.concatenate([density[1:], density[-1:]], axis=0)
    wet_below = jnp.concatenate(
        [entire_ocean_indicator[1:], jnp.zeros_like(entire_ocean_indicator[:1])], axis=0
    )
    strat = jnp.maximum(below - density, 0.0)
    mixing = (
        (MIXING_FLOOR + MIXING_SPAN / (1.0 + STRATIFICATION * strat))
        * entire_ocean_indicator
        * wet_below
    )
    return jnp.stack([dynamics_full[0], dynamics_full[1], dynamics_full[2], mixing], axis=0)


def absorption(arriving_constituents, lit_in):
    wet_centre = (lit_in > 0).astype(jnp.float32)
    surface = lit_in[0]
    pigment = jnp.abs(arriving_constituents[2]) + jnp.abs(arriving_constituents[3])
    absorb = WATER_ABSORB + PIGMENT_ABSORB * pigment
    column = jnp.cumsum(absorb, axis=0)
    heating = surface * (jnp.exp(absorb - column) - jnp.exp(-column)) * wet_centre
    middle = surface * jnp.exp(0.5 * absorb - column)
    return (heating, middle)


def biotic_source_terms(arriving_constituents, thermal_state_grid, layer_centre_irradiance):
    nitrate, ammonium, small_phyto, large_phyto = (
        arriving_constituents[0],
        arriving_constituents[1],
        arriving_constituents[2],
        arriving_constituents[3],
    )
    grazers, small_detritus, large_detritus = (
        arriving_constituents[4],
        arriving_constituents[5],
        arriving_constituents[6],
    )
    nitrate_size = jnp.abs(nitrate)
    ammonium_size = jnp.abs(ammonium)
    light_limit = layer_centre_irradiance / (layer_centre_irradiance + LIGHT_HALF)
    thermal_change_per_step = jnp.exp(THERMAL_GAIN_PER * thermal_state_grid)
    small_common = (
        GROWTH_SMALL
        * thermal_change_per_step
        * light_limit
        * small_phyto
        / (NUTRIENT_HALF_SMALL + nitrate_size + ammonium_size)
    )
    large_common = (
        GROWTH_LARGE
        * thermal_change_per_step
        * light_limit
        * large_phyto
        / (NUTRIENT_HALF_LARGE + nitrate_size + ammonium_size)
    )
    small_nitrate = small_common * nitrate_size
    small_ammonium = small_common * ammonium_size
    large_nitrate = large_common * nitrate_size
    large_ammonium = large_common * ammonium_size
    prey = jnp.abs(small_phyto) + jnp.abs(large_phyto)
    graze_factor = GRAZING_RATE * grazers / (GRAZING_HALF + prey)
    graze_small = graze_factor * small_phyto
    graze_large = graze_factor * large_phyto
    remin = REMINERAL_SMALL * small_detritus + REMINERAL_LARGE * large_detritus
    nitrify = NITRIFICATION * ammonium
    growth = small_nitrate + small_ammonium + large_nitrate + large_ammonium
    tend_nitrate = nitrify - small_nitrate - large_nitrate
    tend_ammonium = remin + EXCRETION * grazers - nitrify - small_ammonium - large_ammonium
    tend_small = small_nitrate + small_ammonium - graze_small - PHYTO_DEATH * small_phyto
    tend_large = large_nitrate + large_ammonium - graze_large - PHYTO_DEATH * large_phyto
    tend_grazers = (
        ASSIMILATION * (graze_small + graze_large)
        - EXCRETION * grazers
        - ZOOPLANKTON_DEATH * grazers
    )
    tend_small_det = (
        PHYTO_DEATH * small_phyto
        + (1.0 - ASSIMILATION) * graze_small
        - REMINERAL_SMALL * small_detritus
    )
    tend_large_det = (
        PHYTO_DEATH * large_phyto
        + ZOOPLANKTON_DEATH * grazers
        + (1.0 - ASSIMILATION) * graze_large
        - REMINERAL_LARGE * large_detritus
    )
    tend_oxygen = OXYGEN_YIELD * growth - OXYGEN_DEMAND * (remin + 2.0 * nitrify)
    return jnp.stack(
        [
            tend_nitrate,
            tend_ammonium,
            tend_small,
            tend_large,
            tend_grazers,
            tend_small_det,
            tend_large_det,
            tend_oxygen,
        ],
        axis=0,
    )


def dynamics_update(dynamics_full, entire_ocean_indicator, heating, row_start, total_rows):
    wet_centre = interior(entire_ocean_indicator)
    density = ocean_water_mass_per_volume(
        dynamics_full[2], dynamics_full[3], entire_ocean_indicator
    )
    pressure = GRAVITY_STEP * jnp.cumsum(density, axis=0)
    force_east, force_north = pressure_force(pressure, entire_ocean_indicator)
    row_count = dynamics_full.shape[3] - 2
    row_index = (jnp.arange(row_count, dtype=jnp.int32) + row_start + 1).astype(jnp.float32)
    coriolis = CORIOLIS_BASE + CORIOLIS_SLOPE * row_index / total_rows
    earlier = dynamics_full[4:8]
    diffused = laplacian(earlier, entire_ocean_indicator)
    carried = advection(
        dynamics_full[0], dynamics_full[1], dynamics_full[2:4], entire_ocean_indicator
    )
    now_centre = interior(dynamics_full[0:4])
    tend_east = coriolis * now_centre[1] - force_east + VISCOSITY * diffused[0]
    tend_north = -coriolis * now_centre[0] - force_north + VISCOSITY * diffused[1]
    tend_temp = -carried[0] + DIFFUSION * diffused[2] + HEATING_GAIN * heating
    tend_salt = -carried[1] + DIFFUSION * diffused[3]
    tendency = jnp.stack([tend_east, tend_north, tend_temp, tend_salt], axis=0)
    earlier_centre = interior(earlier)
    after = earlier_centre + 2.0 * TIME_STEP * tendency * wet_centre
    filtered = now_centre + ASSELIN_GAIN * (earlier_centre - 2.0 * now_centre + after) * wet_centre
    return jnp.concatenate([after, filtered], axis=0)


def tracer_update(tracers_full, flow_full, entire_ocean_indicator, middle):
    wet_centre = interior(entire_ocean_indicator)
    centre = interior(tracers_full)
    carried = advection(flow_full[0], flow_full[1], tracers_full, entire_ocean_indicator)
    spread = laplacian(tracers_full, entire_ocean_indicator)
    mixing = interior(flow_full[3])
    below = jnp.concatenate([centre[:, 1:], jnp.zeros_like(centre[:, :1])], axis=1)
    flux_down = mixing * (below - centre)
    flux_above = jnp.concatenate([jnp.zeros_like(flux_down[:, :1]), flux_down[:, :-1]], axis=1)
    vertical = flux_down - flux_above
    react = biotic_source_terms(centre, interior(flow_full[2]), middle)
    return centre + TIME_STEP * (DIFFUSION * spread - carried + vertical + react) * wet_centre


def extend(combined, width):
    widened = extended(combined, (("gx", 2),), width, True)
    result = extended(widened, (("gy", 3),), width, False)
    return result


def advance(padded, is_dynamics, row_start, total_rows):
    fields = padded[:-1]
    lit_full = padded[-1]
    entire_ocean_indicator = (lit_full > 0).astype(jnp.float32)

    def flow_source(fields_in, wet_in):
        return make_flow(fields_in, wet_in)

    def flow_empty(fields_in, wet_in):
        return jnp.zeros((4,) + wet_in.shape, jnp.float32)

    flow_out = lax.cond(is_dynamics, flow_source, flow_empty, fields, entire_ocean_indicator)

    def light_empty(fields_in, lit_in):
        blank = jnp.zeros(interior(lit_in).shape, jnp.float32)
        return (blank, blank)

    def light_source(fields_in, lit_in):
        return absorption(interior(fields_in), interior(lit_in))

    heat_out, middle = lax.cond(is_dynamics, light_empty, light_source, fields, lit_full)
    partner_flow = broadcast(flow_out, "comp", 0)
    heating = broadcast(heat_out, "comp", 1)

    def run_dynamics(fields_in, flow_in, heat_in, middle_in):
        return dynamics_update(fields_in, entire_ocean_indicator, heat_in, row_start, total_rows)

    def run_tracers(fields_in, flow_in, heat_in, middle_in):
        return tracer_update(fields_in, flow_in, entire_ocean_indicator, middle_in)

    return lax.cond(is_dynamics, run_dynamics, run_tracers, fields, partner_flow, heating, middle)


def local(ocean_state, irradiance, land_mask, bottom_level):
    depth_index = jnp.arange(ocean_state.shape[1], dtype=jnp.int32)[:, None, None]
    wet_cells = ((land_mask[None] == 1) & (depth_index < bottom_level[None])).astype(jnp.float32)
    lit_wet = irradiance[None] * wet_cells
    is_dynamics = lax.axis_index("comp") == 0
    local_rows = ocean_state.shape[3]
    total_rows = local_rows * lax.axis_size("gy")
    own_first_row = lax.axis_index("gy") * local_rows
    current = ocean_state
    for step_index in range(STEPS):
        padded = extend(jnp.concatenate([current, lit_wet[None]], axis=0), 1)
        current = advance(padded, is_dynamics, own_first_row - 1, total_rows)
    return current


def solution(mesh):
    return jax.shard_map(
        local,
        mesh=mesh,
        in_specs=(P("comp", None, "gx", "gy"), P("gx", "gy"), P("gx", "gy"), P("gx", "gy")),
        out_specs=P("comp", None, "gx", "gy"),
        check_vma=False,
    )
```

profile of v0, /device:TPU:1, one launch (start us, length us, event | category | flops | bytes accessed | tf_op | source)
XLA Modules:
  0.0 218.2 jit_solution(1290906092246897796)
XLA Ops:
  6.5 0.7 broadcast_compare_fusion
  7.3 0.7 fusion.157
  8.0 1.1 fusion.155
  9.0 4.4 %collective-permute-start = (f32[9,8,1,128]{3,2,1,0:T(1,128)S(1)}, f32[9,8,1,128]{3,2,1,0:T(1,128)S(1)}, u32[]{:S(2)}, u32[]{:S(2)}) collective-permute-start(f32[9,8,1,128]{3,2,1,0:T(1,128)S(1)} %get-tuple-element.192), channel_id=1, source_target_pairs={{0,1},{1,2},{2,3},{3,4},{4,5},{5,6},{6,7},{7,8},{8,9},{9,10},{10,1... | collective-permute-start | bytes 110600 | tf_op jit(solution)/shard_map/ppermute | solution.py:50
  13.4 17.7 %collective-permute-start.1 = (f32[9,8,1,128]{3,2,1,0:T(1,128)S(1)}, f32[9,8,1,128]{3,2,1,0:T(1,128)S(1)}, u32[]{:S(2)}, u32[]{:S(2)}) collective-permute-start(f32[9,8,1,128]{3,2,1,0:T(1,128)S(1)} %get-tuple-element.193), channel_id=1, source_target_pairs={{1,0},{2,1},{3,2},{4,3},{5,4},{6,5},{7,6},{8,7},{9,8},{10,9},{11,1... | collective-permute-start | bytes 110600 | tf_op jit(solution)/shard_map/ppermute | solution.py:51
  31.1 1.0 collective-permute-done.1
  32.4 4.4 %collective-permute-start.2 = (f32[9,8,6,1]{3,2,1,0:T(8,128)S(1)}, f32[9,8,6,1]{3,2,1,0:T(8,128)S(1)}, u32[]{:S(2)}, u32[]{:S(2)}) collective-permute-start(f32[9,8,6,1]{3,2,1,0:T(8,128)S(1)} %get-tuple-element.188), channel_id=1, source_target_pairs={{0,64},{64,128},{128,192},{192,256},{256,320},{320,384},{384,448},... | collective-permute-start | bytes 5192 | tf_op jit(solution)/shard_map/ppermute | solution.py:50
  36.8 1.3 collective-permute-start.3
  38.1 3.4 %collective-permute-done.2 = f32[9,8,6,1]{3,2,1,0:T(8,128)S(1)} collective-permute-done((f32[9,8,6,1]{3,2,1,0:T(8,128)S(1)}, f32[9,8,6,1]{3,2,1,0:T(8,128)S(1)}, u32[]{:S(2)}, u32[]{:S(2)}) %collective-permute-start.2) | collective-permute-done | bytes 1760 | tf_op jit(solution)/shard_map/ppermute | solution.py:50
  41.5 8.6 %collective-permute-done.3 = f32[9,8,6,1]{3,2,1,0:T(8,128)S(1)} collective-permute-done((f32[9,8,6,1]{3,2,1,0:T(8,128)S(1)}, f32[9,8,6,1]{3,2,1,0:T(8,128)S(1)}, u32[]{:S(2)}, u32[]{:S(2)}) %collective-permute-start.3) | collective-permute-done | bytes 1760 | tf_op jit(solution)/shard_map/ppermute | solution.py:51
  50.8 0.7 broadcast_select_fusion.1
  51.9 7.9 %psum.29 = f32[8,4,128]{2,1,0:T(4,128)S(1)} all-reduce(f32[8,4,128]{2,1,0:T(4,128)S(1)} %broadcast_select_fusion.3), channel_id=1, replica_groups=mesh['comp'=2,'gy'=8,'gx'=64] {'comp'}, use_global_device_ids=true, to_apply=%region_6.7 | all-reduce | flops 4096 | bytes 32768 | tf_op jit(solution)/shard_map/psum | solution.py:58
  59.7 52.0 %all-reduce.9.cloned.1.call-done = f32[4,8,6,130]{3,2,1,0:T(8,128)} async-done(((f32[4,8,6,130]{3,2,1,0:T(8,128)}), f32[4,8,6,130]{3,2,1,0:T(8,128)}) %all-reduce.9.cloned.1.call-update) | async-done | bytes 99856 | tf_op jit(solution)/shard_map/psum | solution.py:58
  111.8 4.4 %conditional.8 = (f32[8,8,4,128]{3,2,1,0:T(4,128)S(1)}) conditional(s32[]{:T(128)} %convert_element_type.37, (f32[8,8,6,130]{3,2,1,0:T(8,128)S(1)}, f32[8,6,130]{2,1,0:T(8,128)S(1)}, f32[4,8,6,130]{3,2,1,0:T(8,128)}, f32[8,4,128]{2,1,0:T(4,128)S(1)}) %tuple.49, (f32[8,8,6,130]{3,2,1,0:T(8,128)S(1)}, s32[]{:T(128)}, f32[8,6,130]{2,1,0:T(8,128)S(1)}, ...), branch_computations={%region_7.8_spmd, %region_8.10_spmd} | conditional | flops 1789951 | bytes 4754520 | solution.py:308
  111.8 1.0 slice_bitcast_fusion.4
  114.0 0.6 copy-done.1
  114.9 0.7 copy-done.2
  116.3 1.9 collective-permute-start.4
  118.2 5.6 %collective-permute-start.5 = (f32[9,8,1,128]{3,2,1,0:T(1,128)S(1)}, f32[9,8,1,128]{3,2,1,0:T(1,128)S(1)}, u32[]{:S(2)}, u32[]{:S(2)}) collective-permute-start(f32[9,8,1,128]{3,2,1,0:T(1,128)S(1)} %get-tuple-element.191), channel_id=1, source_target_pairs={{1,0},{2,1},{3,2},{4,3},{5,4},{6,5},{7,6},{8,7},{9,8},{10,9},{11,1... | collective-permute-start | bytes 110600 | tf_op jit(solution)/shard_map/ppermute | solution.py:51
  123.8 1.0 collective-permute-done.5
  125.1 4.3 %collective-permute-start.6 = (f32[9,8,6,1]{3,2,1,0:T(8,128)S(1)}, f32[9,8,6,1]{3,2,1,0:T(8,128)S(1)}, u32[]{:S(2)}, u32[]{:S(2)}) collective-permute-start(f32[9,8,6,1]{3,2,1,0:T(8,128)S(1)} %get-tuple-element.186), channel_id=1, source_target_pairs={{0,64},{64,128},{128,192},{192,256},{256,320},{320,384},{384,448},... | collective-permute-start | bytes 5192 | tf_op jit(solution)/shard_map/ppermute | solution.py:50
  129.4 1.3 collective-permute-start.7
  130.7 3.7 %collective-permute-done.6 = f32[9,8,6,1]{3,2,1,0:T(8,128)S(1)} collective-permute-done((f32[9,8,6,1]{3,2,1,0:T(8,128)S(1)}, f32[9,8,6,1]{3,2,1,0:T(8,128)S(1)}, u32[]{:S(2)}, u32[]{:S(2)}) %collective-permute-start.6) | collective-permute-done | bytes 1760 | tf_op jit(solution)/shard_map/ppermute | solution.py:50
  134.4 8.2 %collective-permute-done.7 = f32[9,8,6,1]{3,2,1,0:T(8,128)S(1)} collective-permute-done((f32[9,8,6,1]{3,2,1,0:T(8,128)S(1)}, f32[9,8,6,1]{3,2,1,0:T(8,128)S(1)}, u32[]{:S(2)}, u32[]{:S(2)}) %collective-permute-start.7) | collective-permute-done | bytes 1760 | tf_op jit(solution)/shard_map/ppermute | solution.py:51
  143.4 0.7 broadcast_select_fusion
  144.4 3.4 %psum.31 = f32[8,4,128]{2,1,0:T(4,128)S(1)} all-reduce(f32[8,4,128]{2,1,0:T(4,128)S(1)} %broadcast_select_fusion.2), channel_id=1, replica_groups=mesh['comp'=2,'gy'=8,'gx'=64] {'comp'}, use_global_device_ids=true, to_apply=%region_16.17 | all-reduce | flops 4096 | bytes 32768 | tf_op jit(solution)/shard_map/psum | solution.py:58
  147.8 58.5 %all-reduce.11.cloned.1.call-done = f32[4,8,6,130]{3,2,1,0:T(8,128)} async-done(((f32[4,8,6,130]{3,2,1,0:T(8,128)}), f32[4,8,6,130]{3,2,1,0:T(8,128)}) %all-reduce.11.cloned.1.call-update) | async-done | bytes 99856 | tf_op jit(solution)/shard_map/psum | solution.py:58
  206.3 4.4 %conditional.11 = (f32[8,8,4,128]{3,2,1,0:T(4,128)S(1)}) conditional(s32[]{:T(128)} %convert_element_type.37, (f32[8,8,6,130]{3,2,1,0:T(8,128)S(1)}, f32[8,6,130]{2,1,0:T(8,128)S(1)}, f32[4,8,6,130]{3,2,1,0:T(8,128)}, f32[8,4,128]{2,1,0:T(4,128)S(1)}) %tuple.55, (f32[8,8,6,130]{3,2,1,0:T(8,128)S(1)}, s32[]{:T(128)}, f32[8,6,130]{2,1,0:T(8,128)S(1)}, ...), branch_computations={%region_17.18_spmd, %region_18.20_spmd} | conditional | flops 1789951 | bytes 4754520 | solution.py:308
  206.3 1.0 slice_bitcast_fusion.11
  208.6 0.6 copy-done.3
  209.4 0.7 copy-done.4
  210.7 0.6 copy-done.8
  (72 shorter events, 7.0 us)
Async XLA Ops:
  6.5 0.7 copy-start.9
  6.5 25.6 %copy-start = (f32[8,8,4,128]{3,2,1,0:T(4,128)S(1)}, f32[8,8,4,128]{3,2,1,0:T(4,128)}, u32[]{:S(2)}) copy-start(f32[8,8,4,128]{3,2,1,0:T(4,128)} %param.16) | copy-start | bytes 393220
  6.5 105.2 %all-reduce.9.cloned.1.call-start = ((), (), s32[]{:S(2)}) async-start(), calls=%async_computation | async-start | bytes 524288 | tf_op jit(solution)/shard_map/psum | solution.py:58
  9.0 22.1 %collective-permute-start = (f32[9,8,1,128]{3,2,1,0:T(1,128)S(1)}, f32[9,8,1,128]{3,2,1,0:T(1,128)S(1)}, u32[]{:S(2)}, u32[]{:S(2)}) collective-permute-start(f32[9,8,1,128]{3,2,1,0:T(1,128)S(1)} %get-tuple-element.192), channel_id=1, source_target_pairs={{0,1},{1,2},{2,3},{3,4},{4,5},{5,6},{6,7},{7,8},{8,9},{9,10},{10,1... | collective-permute-start | bytes 110600 | tf_op jit(solution)/shard_map/ppermute | solution.py:50
  13.4 18.7 %collective-permute-start.1 = (f32[9,8,1,128]{3,2,1,0:T(1,128)S(1)}, f32[9,8,1,128]{3,2,1,0:T(1,128)S(1)}, u32[]{:S(2)}, u32[]{:S(2)}) collective-permute-start(f32[9,8,1,128]{3,2,1,0:T(1,128)S(1)} %get-tuple-element.193), channel_id=1, source_target_pairs={{1,0},{2,1},{3,2},{4,3},{5,4},{6,5},{7,6},{8,7},{9,8},{10,9},{11,1... | collective-permute-start | bytes 110600 | tf_op jit(solution)/shard_map/ppermute | solution.py:51
  32.4 9.1 %collective-permute-start.2 = (f32[9,8,6,1]{3,2,1,0:T(8,128)S(1)}, f32[9,8,6,1]{3,2,1,0:T(8,128)S(1)}, u32[]{:S(2)}, u32[]{:S(2)}) collective-permute-start(f32[9,8,6,1]{3,2,1,0:T(8,128)S(1)} %get-tuple-element.188), channel_id=1, source_target_pairs={{0,64},{64,128},{128,192},{192,256},{256,320},{320,384},{384,448},... | collective-permute-start | bytes 5192 | tf_op jit(solution)/shard_map/ppermute | solution.py:50
  36.8 13.3 %collective-permute-start.3 = (f32[9,8,6,1]{3,2,1,0:T(8,128)S(1)}, f32[9,8,6,1]{3,2,1,0:T(8,128)S(1)}, u32[]{:S(2)}, u32[]{:S(2)}) collective-permute-start(f32[9,8,6,1]{3,2,1,0:T(8,128)S(1)} %get-tuple-element.189), channel_id=1, source_target_pairs={{64,0},{128,64},{192,128},{256,192},{320,256},{384,320},{448,384},... | collective-permute-start | bytes 5192 | tf_op jit(solution)/shard_map/ppermute | solution.py:51
  51.6 154.7 %all-reduce.11.cloned.1.call-start = ((), (), s32[]{:S(2)}) async-start(), calls=%async_computation.1 | async-start | bytes 524288 | tf_op jit(solution)/shard_map/psum | solution.py:58
  114.0 0.7 copy-start.1
  114.7 0.9 copy-start.2
  114.8 0.9 slice-start
  116.3 7.5 %collective-permute-start.4 = (f32[9,8,1,128]{3,2,1,0:T(1,128)S(1)}, f32[9,8,1,128]{3,2,1,0:T(1,128)S(1)}, u32[]{:S(2)}, u32[]{:S(2)}) collective-permute-start(f32[9,8,1,128]{3,2,1,0:T(1,128)S(1)} %get-tuple-element.190), channel_id=1, source_target_pairs={{0,1},{1,2},{2,3},{3,4},{4,5},{5,6},{6,7},{7,8},{8,9},{9,10},{10,1... | collective-permute-start | bytes 110600 | tf_op jit(solution)/shard_map/ppermute | solution.py:50
  118.2 6.6 %collective-permute-start.5 = (f32[9,8,1,128]{3,2,1,0:T(1,128)S(1)}, f32[9,8,1,128]{3,2,1,0:T(1,128)S(1)}, u32[]{:S(2)}, u32[]{:S(2)}) collective-permute-start(f32[9,8,1,128]{3,2,1,0:T(1,128)S(1)} %get-tuple-element.191), channel_id=1, source_target_pairs={{1,0},{2,1},{3,2},{4,3},{5,4},{6,5},{7,6},{8,7},{9,8},{10,9},{11,1... | collective-permute-start | bytes 110600 | tf_op jit(solution)/shard_map/ppermute | solution.py:51
  125.1 9.3 %collective-permute-start.6 = (f32[9,8,6,1]{3,2,1,0:T(8,128)S(1)}, f32[9,8,6,1]{3,2,1,0:T(8,128)S(1)}, u32[]{:S(2)}, u32[]{:S(2)}) collective-permute-start(f32[9,8,6,1]{3,2,1,0:T(8,128)S(1)} %get-tuple-element.186), channel_id=1, source_target_pairs={{0,64},{64,128},{128,192},{192,256},{256,320},{320,384},{384,448},... | collective-permute-start | bytes 5192 | tf_op jit(solution)/shard_map/ppermute | solution.py:50
  129.4 13.2 %collective-permute-start.7 = (f32[9,8,6,1]{3,2,1,0:T(8,128)S(1)}, f32[9,8,6,1]{3,2,1,0:T(8,128)S(1)}, u32[]{:S(2)}, u32[]{:S(2)}) collective-permute-start(f32[9,8,6,1]{3,2,1,0:T(8,128)S(1)} %get-tuple-element.187), channel_id=1, source_target_pairs={{64,0},{128,64},{192,128},{256,192},{320,256},{384,320},{448,384},... | collective-permute-start | bytes 5192 | tf_op jit(solution)/shard_map/ppermute | solution.py:51
  208.5 0.7 copy-start.3
  209.2 0.9 copy-start.4
  209.3 0.9 slice-start.1
  210.7 0.7 copy-start.8
Sparse Core Ops, SparseCore 0:
  51.7 60.0 all-reduce.8
  144.3 61.9 all-reduce.10
where the time goes:
time: 219 us; the launch traced here: 218 us
  waiting for transfers between devices  137 us (63%)
  starting transfers between devices  40.9 us (19%)
  between operations  13.7 us (6%)
  blocking collectives  11.3 us (5%)
  other arithmetic  9.11 us (4%)
  local copies, waits for them, and re-layouts  6.43 us (3%)
    psum x2, waiting for transfers between devices, broadcast(): return lax.psum(jnp.where(mine, shard, jnp.zeros_like(shard)), axis)  111 us
    ppermute x4, starting transfers between devices, extended(): after = lax.ppermute(leading, axis, down)  25.9 us
    ppermute x4, waiting for transfers between devices, extended(): after = lax.ppermute(leading, axis, down)  18.9 us
    ppermute x4, starting transfers between devices, extended(): before = lax.ppermute(last, axis, up)  15 us
    psum x2, blocking collectives, broadcast(): return lax.psum(jnp.where(mine, shard, jnp.zeros_like(shard)), axis)  11.3 us
    ppermute x4, waiting for transfers between devices, extended(): before = lax.ppermute(last, axis, up)  7.12 us
  transfers between devices with their start and end apart: 10, of which 8 were waited for; matrix products, arithmetic and copies ran while one was open for 0% of the time, Pallas kernels for 0%

commit v1 on v0

v1 whole, which is shorter than its diff:
```python
import functools

import jax
import jax.numpy as jnp
from jax import lax
from jax.experimental import pallas as pl
from jax.experimental.pallas import tpu as pltpu
from jax.sharding import PartitionSpec as P

MESH = pl.DeviceIdType.MESH

SOUTH, NORTH, SW, SE, NW, NE = range(6)
OWN = 2
LEV, LANES = 8, 128


def roll(value, shift, axis):
    return pltpu.roll(value, shift % value.shape[axis], axis)


def lanes(value, shift):
    return roll(value, shift, value.ndim - 1)


def levels(value, shift):
    return roll(value, shift, value.ndim - 2)


def iota(dim):
    return lax.broadcasted_iota(jnp.int32, (LEV, LANES), dim)


def level_sum(value):
    k = iota(0)
    for shift in (1, 2, 4):
        value = value + jnp.where(k >= shift, levels(value, shift), 0.0)
    return value


def density(temp, salt, wet):
    return (0.8 * salt - 0.2 * temp) * wet


def pressure_of(temp, salt, wet):
    return 0.1 * level_sum(density(temp, salt, wet))


def mixing_of(temp, salt, wet):
    rho = density(temp, salt, wet)
    strat = jnp.maximum(levels(rho, -1) - rho, 0.0)
    wet_below = jnp.where(iota(0) == LEV - 1, 0.0, levels(wet, -1))
    return (0.05 + 1.0 / (1.0 + 4.0 * strat)) * wet * wet_below


def absorbed(small, large):
    absorb = 0.08 + 0.05 * (jnp.abs(small) + jnp.abs(large))
    return absorb, level_sum(absorb)


def surface_of(lit):
    return jnp.broadcast_to(lit[0:1, :], (LEV, LANES))


def heating_of(small, large, lit, wet):
    absorb, column = absorbed(small, large)
    return surface_of(lit) * (jnp.exp(absorb - column) - jnp.exp(-column)) * wet


def light_of(small, large, lit):
    absorb, column = absorbed(small, large)
    return surface_of(lit) * jnp.exp(0.5 * absorb - column)


def gradients(p, wet):
    pc, pe, pw, pn, ps = p
    _, we, ww, wn, ws = wet
    return 0.5 * (we * (pe - pc) + ww * (pc - pw)), 0.5 * (wn * (pn - pc) + ws * (pc - ps))


def spread_of(field, wet):
    c, e, w, n, s = field
    _, we, ww, wn, ws = wet
    return we * (e - c) + ww * (w - c) + wn * (n - c) + ws * (s - c)


def faces(u, v, wet):
    (uc, ue, uw), (vc, vn, vs) = u, v
    _, we, ww, wn, ws = wet
    return 0.25 * (uc + ue) * we, 0.25 * (uc + uw) * ww, 0.25 * (vc + vn) * wn, 0.25 * (vc + vs) * ws


def carried_of(field, face):
    c, e, w, n, s = field
    fe, fw, fn, fs = face
    return fe * (c + e) - fw * (c + w) + fn * (c + n) - fs * (c + s)


def pick(five, index):
    return tuple(part[index] for part in five)


def step_speeds(now, before, p, wet, coriolis):
    force_east, force_north = gradients(p, wet)
    u, v = now[0][0], now[0][1]
    du = coriolis * v - force_east + 0.2 * spread_of(pick(before, 0), wet)
    dv = -coriolis * u - force_north + 0.2 * spread_of(pick(before, 1), wet)
    return before[0][0] + 0.2 * du * wet[0], before[0][1] + 0.2 * dv * wet[0]


def step_heat_salt(now, before, wet, heating):
    u = (now[0][0], now[1][0], now[2][0])
    v = (now[0][1], now[3][1], now[4][1])
    face = faces(u, v, wet)
    dt = -carried_of(pick(now, 2), face) + 0.2 * spread_of(pick(before, 2), wet) + 3.0 * heating
    ds = -carried_of(pick(now, 3), face) + 0.2 * spread_of(pick(before, 3), wet)
    return before[0][2] + 0.2 * dt * wet[0], before[0][3] + 0.2 * ds * wet[0]


def filtered(now, before, after, wet):
    return now + 0.1 * (before - 2.0 * now + after) * wet


def transported(field, u, v, wet):
    c, e, w, n, s = field
    _, we, ww, wn, ws = wet
    fe, fw, fn, fs = faces(u, v, wet)
    le, lw, ln, ls = 0.2 * we, 0.2 * ww, 0.2 * wn, 0.2 * ws
    own = (le + fe) + (lw - fw) + (ln + fn) + (ls - fs)
    return (le - fe) * e + (lw + fw) * w + (ln - fn) * n + (ls + fs) * s - own * c


def mixed(c, kappa):
    down = kappa * (levels(c, -1) - c)
    return down - levels(down, 1)


def growth_of(nitrate, ammonium, small, large, temp, light):
    rate = jnp.exp(0.06 * temp) * (light / (light + 0.5))
    both = jnp.abs(nitrate) + jnp.abs(ammonium)
    return 0.6 * rate * small / (0.2 + both), 0.9 * rate * large / (0.8 + both)


def reactions(c, temp, light):
    nn, na = jnp.abs(c[0]), jnp.abs(c[1])
    small, large = growth_of(c[0], c[1], c[2], c[3], temp, light)
    sn, sa, ln, la = small * nn, small * na, large * nn, large * na
    graze = 0.8 * c[4] / (1.0 + jnp.abs(c[2]) + jnp.abs(c[3]))
    gs, gl = graze * c[2], graze * c[3]
    remin = 0.3 * c[5] + 0.1 * c[6]
    nitrify = 0.2 * c[1]
    return jnp.stack(
        [
            nitrify - sn - ln,
            remin + 0.1 * c[4] - nitrify - sa - la,
            sn + sa - gs - 0.1 * c[2],
            ln + la - gl - 0.1 * c[3],
            0.7 * (gs + gl) - 0.1 * c[4] - 0.15 * c[4],
            0.1 * c[2] + 0.3 * gs - 0.3 * c[5],
            0.1 * c[3] + 0.15 * c[4] + 0.3 * gl - 0.1 * c[6],
            1.3 * (sn + sa + ln + la) - (remin + 2.0 * nitrify),
        ]
    )


def plant_reactions(c, temp, light):
    both = jnp.abs(c[0]) + jnp.abs(c[1])
    small, large = growth_of(c[0], c[1], c[2], c[3], temp, light)
    graze = 0.8 * c[4] / (1.0 + jnp.abs(c[2]) + jnp.abs(c[3]))
    return jnp.stack([small * both - graze * c[2] - 0.1 * c[2], large * both - graze * c[3] - 0.1 * c[3]])


def row_edges(strip):
    slot = iota(1) % 4
    return jnp.where(slot == 2, lanes(strip, 64), strip)


def around(columns, edges, col):
    lane = iota(1)
    c = columns(col)
    edge = lanes(edges, -(4 * (col - 1) + 2))
    north = lanes(jnp.where(lane == 0, edge, c), -1)
    south = lanes(jnp.where(lane == LANES - 1, edge, c), 1)
    return c, columns(col + 1), columns(col - 1), north, south


def around_strip(strip):
    return strip, lanes(strip, -4), lanes(strip, 4), lanes(strip, -1), lanes(strip, 1)


def wet_faces(wet):
    c, e, w, n, s = wet
    return c, c * e, c * w, c * n, c * s


def kernel(
    gy_size, gx_size, state, irr, land, bottom, out,
    raw, irr_v, land_v, bottom_v, mine, other, packs, strips_in, strip, edges, strip_o, edges_o,
    wet, press, next_d, next_t, nstrip, nedges,
    load_sem, send_sem, recv_sem,
):
    comp, gy, gx = (lax.axis_index(a) for a in ("comp", "gy", "gx"))
    east, west = lax.rem(gx + 1, gx_size), lax.rem(gx + gx_size - 1, gx_size)
    up, down = lax.rem(gy + 1, gy_size), lax.rem(gy + gy_size - 1, gy_size)
    twin = 1 - comp
    places = [(up, east), (up, west), (down, east), (down, west), (up, gx), (down, gx), (gy, east), (gy, west)]

    barrier = pltpu.get_barrier_semaphore()
    for y, x in places:
        for c in (comp, twin):
            pl.semaphore_signal(barrier, inc=1, device_id=(c, y, x), device_id_type=MESH)
    pl.semaphore_signal(barrier, inc=1, device_id=(twin, gy, gx), device_id_type=MESH)

    loads = [
        pltpu.make_async_copy(src, dst, load_sem.at[i])
        for i, (src, dst) in enumerate([(irr, irr_v), (land, land_v), (bottom, bottom_v), (state, raw)])
    ]
    for load in loads:
        load.start()
    for load in loads:
        load.wait()

    lane, k = iota(1), iota(0)
    slot, quad = lane % 4, lane // 4

    for x in range(4):
        is_wet = (land_v[x : x + 1, :] == 1) & (k < bottom_v[x : x + 1, :])
        mine[8, OWN + x] = jnp.where(is_wet, jnp.broadcast_to(irr_v[x : x + 1, :], (LEV, LANES)), 0.0)
        for f in range(8):
            mine[f, OWN + x] = raw[pl.ds(f * 32 + x, 8, stride=4), :]
    rows = jnp.zeros((LEV, LANES), jnp.float32)
    lit_rows = jnp.zeros((LEV, LANES), jnp.float32)
    for x in range(4):
        for f in range(8):
            rows = jnp.where(quad == 4 * f + x, lanes(mine[f, OWN + x], 16 * f + 4 * x + 2), rows)
        lit_rows = jnp.where(quad == x, lanes(mine[8, OWN + x], 4 * x + 2), lit_rows)
    packs[0] = jnp.where(slot < 2, rows, lanes(lit_rows, 2))
    packs[1] = jnp.where(slot < 2, lanes(lit_rows, -2), rows)

    pl.semaphore_wait(barrier, 2 * len(places) + 1)

    def remote(index, src, dst, target):
        return pltpu.make_async_remote_copy(
            src_ref=src, dst_ref=dst, send_sem=send_sem.at[index], recv_sem=recv_sem.at[index],
            device_id=target, device_id_type=MESH,
        )

    ways = [(SW, 0, up, east), (SE, 0, up, west), (NW, 1, down, east), (NE, 1, down, west), (SOUTH, 0, up, gx), (NORTH, 1, down, gx)]
    same_rows = [remote(s, packs.at[p], strips_in.at[0, s], (comp, y, x)) for s, p, y, x in ways]
    twin_rows = [remote(6 + s, packs.at[p], strips_in.at[1, s], (twin, y, x)) for s, p, y, x in ways]
    same_cols = [
        remote(12, mine.at[:, 4:6], mine.at[:, 0:2], (comp, gy, east)),
        remote(13, mine.at[:, 2:4], mine.at[:, 6:8], (comp, gy, west)),
    ]
    flow_cols = [
        remote(14, mine.at[0:8, 4:6], other.at[0:8, 0:2], (twin, gy, east)),
        remote(15, mine.at[0:8, 2:4], other.at[0:8, 6:8], (twin, gy, west)),
    ]
    plant_cols = [
        remote(14, mine.at[2:4, 5:6], other.at[2:4, 1:2], (twin, gy, east)),
        remote(15, mine.at[2:4, 2:3], other.at[2:4, 6:7], (twin, gy, west)),
    ]
    flow_own = remote(16, mine.at[0:8, 2:6], other.at[0:8, 2:6], (twin, gy, gx))
    plant_own = remote(16, mine.at[0:5, 2:6], other.at[0:5, 2:6], (twin, gy, gx))

    dyn_sends = same_rows[:4] + twin_rows[:4] + same_rows[4:] + twin_rows[4:] + same_cols + flow_cols + [flow_own]
    trc_sends = same_rows + twin_rows[4:] + same_cols + plant_cols + [plant_own]

    @pl.when(comp == 0)
    def _():
        for copy in dyn_sends:
            copy.start()

    @pl.when(comp == 1)
    def _():
        for copy in trc_sends:
            copy.start()

    no_south, no_north = gy == 0, gy == gy_size - 1
    col3 = quad % 4 == 3
    low = lane < 64
    middle = (lane >= 32) & (lane < 96)
    inner = (lane % 64 >= 4) & (lane % 64 < 20)

    def build(own_rows, arrived, fields, store):
        south = jnp.where(slot < 2, arrived[SOUTH], own_rows)
        north = lanes(jnp.where(slot < 2, own_rows, arrived[NORTH]), 64)
        se, nw, ne = lanes(arrived[SE], 32), lanes(arrived[NW], 64), lanes(arrived[NE], 96)
        halves = (jnp.where(low, south, north), jnp.where(low, north, south))
        corners = (
            jnp.where(col3, jnp.where(low, arrived[SW], nw), jnp.where(middle, se, ne)),
            jnp.where(col3, jnp.where(low, nw, arrived[SW]), jnp.where(middle, ne, se)),
        )
        for f in fields:
            store(f, jnp.where(inner, lanes(halves[f // 4], 4 - 16 * f), lanes(corners[f // 4], -12 - 16 * f)))

    def strips(lit_sides, own_strip, own_edges, my_fields, other_rows, other_fields):
        def keep(ref, edge_ref):
            def store(f, value):
                ref[f] = value
                edge_ref[f] = row_edges(value)

            return store

        build(own_strip, [strips_in[0, s] for s in range(6)], my_fields, keep(strip, edges))
        lit_in = []
        for s in range(6):
            southern = s in (SOUTH, SW, SE)
            dry = no_south if southern else no_north
            lit_in.append(jnp.where(dry, 0.0, lanes(strips_in[0, s], -2 if southern else 2)))
        build(lit_sides, lit_in, [0], lambda f, value: keep(strip, edges)(8, value))
        build(other_rows, [strips_in[1, s] for s in range(6)], other_fields, keep(strip_o, edges_o))

    def other_own_rows(fields):
        result = jnp.zeros((LEV, LANES), jnp.float32)
        for f in fields:
            for x in range(4):
                result = jnp.where(quad == 4 * f + x, lanes(other[f, OWN + x], 16 * f + 4 * x + 2), result)
        return result

    def wet_everywhere():
        for col in range(8):
            wet[0, col] = (mine[8, col] > 0).astype(jnp.float32)
        wet_strip = (strip[8] > 0).astype(jnp.float32)
        wet_edges = row_edges(wet_strip)
        at = {col: wet_faces(around(lambda c: wet[0, c], wet_edges, col)) for col in range(1, 7)}
        return at, wet_faces(around_strip(wet_strip)), wet_strip

    first_row = gy * LANES
    coriolis_main = 0.3 + 0.4 * (first_row + lane).astype(jnp.float32) / float(gy_size * LANES)
    strip_row = first_row + slot + jnp.where(low, -2, LANES - 2)
    coriolis_strip = 0.3 + 0.4 * strip_row.astype(jnp.float32) / float(gy_size * LANES)

    def store_out(f, x, value):
        out[pl.ds(f * 32 + x, 8, stride=4), :] = value

    @pl.when(comp == 0)
    def _():
        for copy in [flow_own] + plant_cols + same_cols + twin_rows[4:] + same_rows:
            if copy is flow_own:
                plant_own.wait_recv()
            else:
                copy.wait_recv()
        strips(lit_rows, rows, None, range(8), other_own_rows((2, 3)), (2, 3))
        wet_at, wet_h, wet_strip = wet_everywhere()
        for col in range(8):
            press[0, col] = pressure_of(mine[2, col], mine[3, col], wet[0, col])
        press_h = pressure_of(strip[2], strip[3], wet_strip)
        press_e = row_edges(press_h)

        def full_step(now, before, p, wets, coriolis, heating):
            u, v = step_speeds(now, before, p, wets, coriolis)
            t, s = step_heat_salt(now, before, wets, heating)
            after = jnp.stack([u, v, t, s])
            return after, filtered(now[0], before[0], after, wets[0])

        h_now, h_before = around_strip(strip[0:4]), around_strip(strip[4:8])
        h_heat = heating_of(strip_o[2], strip_o[3], strip[8], wet_strip)
        after, filt = full_step(h_now, h_before, around_strip(press_h), wet_h, coriolis_strip, h_heat)
        nstrip[0:4], nstrip[4:8] = after, filt
        nedges[0:4], nedges[4:8] = row_edges(after), row_edges(filt)
        for col in range(1, 7):
            now = around(lambda c: mine[0:4, c], edges[0:4], col)
            before = around(lambda c: mine[4:8, c], edges[4:8], col)
            p = around(lambda c: press[0, c], press_e, col)
            heat = heating_of(other[2, col], other[3, col], mine[8, col], wet[0, col])
            after, filt = full_step(now, before, p, wet_at[col], coriolis_main, heat)
            next_d[0:4, col], next_d[4:8, col] = after, filt
        for col in range(2, 6):
            c = other[0:5, col]
            u = around(lambda c: mine[0, c], edges[0], col)
            v = around(lambda c: mine[1, c], edges[1], col)
            plants = around(lambda c: other[2:4, c], edges_o[2:4], col)
            kappa = mixing_of(mine[2, col], mine[3, col], wet[0, col])
            light = light_of(c[2], c[3], mine[8, col])
            change = transported(plants, u[:3], (v[0], v[3], v[4]), wet_at[col]) + mixed(plants[0], kappa)
            change = change + plant_reactions(c, mine[2, col], light)
            next_t[2:4, col] = plants[0] + 0.1 * change * wet[0, col]
        for col in range(1, 7):
            press[1, col] = pressure_of(next_d[2, col], next_d[3, col], wet[0, col])
        press_e = row_edges(pressure_of(nstrip[2], nstrip[3], wet_strip))
        for col in range(2, 6):
            now = around(lambda c: next_d[0:4, c], nedges[0:4], col)
            before = around(lambda c: next_d[4:8, c], nedges[4:8], col)
            p = around(lambda c: press[1, c], press_e, col)
            heat = heating_of(next_t[2, col], next_t[3, col], mine[8, col], wet[0, col])
            after, filt = full_step(now, before, p, wet_at[col], coriolis_main, heat)
            for f in range(4):
                store_out(f, col - 2, after[f])
                store_out(4 + f, col - 2, filt[f])

    @pl.when(comp == 1)
    def _():
        for copy in [flow_own] + flow_cols + same_cols + twin_rows[4:] + same_rows[4:] + twin_rows[:4] + same_rows[:4]:
            copy.wait_recv()
        strips(lit_rows, rows, None, range(8), other_own_rows(range(8)), range(8))
        wet_at, wet_h, wet_strip = wet_everywhere()
        for col in range(8):
            press[0, col] = pressure_of(other[2, col], other[3, col], wet[0, col])
        press_h = pressure_of(strip_o[2], strip_o[3], wet_strip)
        press_e = row_edges(press_h)

        def tracer_step(c, u, v, wets, temp, salt, lit):
            kappa = mixing_of(temp, salt, wets[0])
            light = light_of(c[0][2], c[0][3], lit)
            change = transported(c, u, v, wets) + mixed(c[0], kappa) + reactions(c[0], temp, light)
            return c[0] + 0.1 * change * wets[0]

        now, before = around_strip(strip_o[0:4]), around_strip(strip_o[4:6])
        u, v = step_speeds(now, before, around_strip(press_h), wet_h, coriolis_strip)
        nedges[8], nedges[9] = row_edges(u), row_edges(v)
        u = (now[0][0], now[1][0], now[2][0])
        v = (now[0][1], now[3][1], now[4][1])
        new = tracer_step(around_strip(strip[0:8]), u, v, wet_h, strip_o[2], strip_o[3], strip[8])
        nedges[0:8] = row_edges(new)
        for col in range(1, 7):
            now = around(lambda c: other[0:4, c], edges_o[0:4], col)
            before = around(lambda c: other[4:8, c], edges_o[4:8], col)
            p = around(lambda c: press[0, c], press_e, col)
            next_d[0, col], next_d[1, col] = step_speeds(now, before, p, wet_at[col], coriolis_main)
            c = around(lambda c: mine[0:8, c], edges[0:8], col)
            if 2 <= col < 6:
                heat = heating_of(c[0][2], c[0][3], mine[8, col], wet[0, col])
                next_d[2, col], next_d[3, col] = step_heat_salt(now, before, wet_at[col], heat)
            u = (now[0][0], now[1][0], now[2][0])
            v = (now[0][1], now[3][1], now[4][1])
            next_t[0:8, col] = tracer_step(c, u, v, wet_at[col], other[2, col], other[3, col], mine[8, col])
        for col in range(2, 6):
            c = around(lambda c: next_t[0:8, c], nedges[0:8], col)
            u = around(lambda c: next_d[0, c], nedges[8], col)
            v = around(lambda c: next_d[1, c], nedges[9], col)
            new = tracer_step(
                c, u[:3], (v[0], v[3], v[4]), wet_at[col], next_d[2, col], next_d[3, col], mine[8, col]
            )
            for f in range(8):
                store_out(f, col - 2, new[f])

    @pl.when(comp == 0)
    def _():
        for copy in dyn_sends:
            copy.wait_send()

    @pl.when(comp == 1)
    def _():
        for copy in trc_sends:
            copy.wait_send()


def solution(mesh):
    gy_size, gx_size = mesh.shape["gy"], mesh.shape["gx"]

    def local(ocean_state, irradiance, land_mask, bottom_level):
        rows = ocean_state.size // LANES
        anywhere = pl.BlockSpec(memory_space=pl.ANY)
        f32 = jnp.float32
        result = pl.pallas_call(
            functools.partial(kernel, gy_size, gx_size),
            out_shape=jax.ShapeDtypeStruct((rows, LANES), f32),
            in_specs=[anywhere] * 4,
            out_specs=pl.BlockSpec(memory_space=pltpu.VMEM),
            scratch_shapes=[
                pltpu.VMEM((rows, LANES), f32),
                pltpu.VMEM((4, LANES), f32),
                pltpu.VMEM((4, LANES), jnp.int32),
                pltpu.VMEM((4, LANES), jnp.int32),
                pltpu.VMEM((9, 8, LEV, LANES), f32),
                pltpu.VMEM((8, 8, LEV, LANES), f32),
                pltpu.VMEM((2, LEV, LANES), f32),
                pltpu.VMEM((2, 6, LEV, LANES), f32),
                pltpu.VMEM((9, LEV, LANES), f32),
                pltpu.VMEM((9, LEV, LANES), f32),
                pltpu.VMEM((8, LEV, LANES), f32),
                pltpu.VMEM((8, LEV, LANES), f32),
                pltpu.VMEM((1, 8, LEV, LANES), f32),
                pltpu.VMEM((2, 8, LEV, LANES), f32),
                pltpu.VMEM((8, 8, LEV, LANES), f32),
                pltpu.VMEM((8, 8, LEV, LANES), f32),
                pltpu.VMEM((8, LEV, LANES), f32),
                pltpu.VMEM((10, LEV, LANES), f32),
                pltpu.SemaphoreType.DMA((4,)),
                pltpu.SemaphoreType.DMA((17,)),
                pltpu.SemaphoreType.DMA((17,)),
            ],
            compiler_params=pltpu.CompilerParams(
                collective_id=0, has_side_effects=True, vmem_limit_bytes=8 * 1024 * 1024
            ),
            name="coupled_steps",
        )(ocean_state.reshape(rows, LANES), irradiance, land_mask, bottom_level)
        return result.reshape(ocean_state.shape)

    return jax.shard_map(
        local,
        mesh=mesh,
        in_specs=(P("comp", None, "gx", "gy"), P("gx", "gy"), P("gx", "gy"), P("gx", "gy")),
        out_specs=P("comp", None, "gx", "gy"),
        check_vma=False,
    )
```

time: 219 us -> 34.1 us (0.16)
  waiting for transfers between devices: 137 us -> 0 us
  starting transfers between devices: 40.9 us -> 0 us
  Pallas kernels: 0 us -> 30.3 us
  between operations: 13.7 us -> 0.01 us
  blocking collectives: 11.3 us -> 0 us
  other arithmetic: 9.11 us -> 0 us
  local copies, waits for them, and re-layouts: 6.43 us -> 3.6 us
    psum x2 -> x0, waiting for transfers between devices: 111 us -> none  [broadcast(): return lax.psum(jnp.where(mine, shard, jnp.zeros_like(shard)), axis)]
    ppermute x8 -> x0, starting transfers between devices: 40.9 us -> none  [the longest x4 25.9 us: extended(): after = lax.ppermute(leading, axis, down)]
    pallas_call x0 -> x1, Pallas kernels: none -> 30.3 us  [local(): pl.pallas_call(functools.partial(kernel, gy_size, gx_size), out_shape=jax...]
    ppermute x8 -> x0, waiting for transfers between devices: 26 us -> none  [the longest x4 18.9 us: extended(): after = lax.ppermute(leading, axis, down)]
    psum x2 -> x0, blocking collectives: 11.3 us -> none  [broadcast(): return lax.psum(jnp.where(mine, shard, jnp.zeros_like(shard)), axis)]
    unnamed x6 -> x9, local copies, waits for them, and re-layouts: 0.66 us -> 3.6 us
    cond x8 -> x0, local copies, waits for them, and re-layouts: 2.63 us -> none
    concatenate x6 -> x0, other arithmetic: 2.52 us -> none  [the longest x4 1.41 us: extended(): shard = jnp.concatenate([before, shard, after], axis=dim)]
  transfers between devices with their start and end apart: 10 -> 0, of which waited for: 8 -> 0; matrix products, arithmetic and copies ran while one was open for 0% -> 0% of each run, Pallas kernels for 0% -> 0%
where the time goes in v1:
time: 34.1 us; the launch traced here: 33.9 us
  Pallas kernels  30.3 us (89%)
  local copies, waits for them, and re-layouts  3.6 us (11%)
    pallas_call x1, Pallas kernels, local(): pl.pallas_call(functools.partial(kernel, gy_size, gx_size), out_shape=jax...  30.3 us
    unnamed x9, local copies, waits for them, and re-layouts  3.6 us

profile of v1, /device:TPU:1, one launch (start us, length us, event | category | flops | bytes accessed | tf_op | source)
XLA Modules:
  0.0 33.9 jit_solution(15967760396551867655)
XLA Ops:
  0.0 0.0 copy-start
  0.0 0.9 %copy-done = f32[8,8,4,128]{3,2,1,0:T(4,128)S(1)} copy-done((f32[8,8,4,128]{3,2,1,0:T(4,128)S(1)}, f32[8,8,4,128]{3,2,1,0:T(4,128)}, u32[]{:S(2)}) %copy-start) | copy-done | bytes 131096
  0.9 0.0 copy-start.1
  0.9 0.7 %copy-done.1 = f32[4,128]{1,0:T(4,128)S(1)} copy-done((f32[4,128]{1,0:T(4,128)S(1)}, f32[4,128]{1,0:T(4,128)}, u32[]{:S(2)}) %copy-start.1) | copy-done | bytes 2072
  1.6 0.0 copy-start.2
  1.6 0.7 %copy-done.2 = s32[4,128]{1,0:T(4,128)S(1)} copy-done((s32[4,128]{1,0:T(4,128)S(1)}, s32[4,128]{1,0:T(4,128)}, u32[]{:S(2)}) %copy-start.2) | copy-done | bytes 2072
  2.3 0.0 copy-start.3
  2.3 0.7 %copy-done.3 = s32[4,128]{1,0:T(4,128)S(1)} copy-done((s32[4,128]{1,0:T(4,128)S(1)}, s32[4,128]{1,0:T(4,128)}, u32[]{:S(2)}) %copy-start.3) | copy-done | bytes 2072
  3.0 30.3 %coupled_steps.1 = f32[256,128]{1,0:T(8,128)S(1)} custom-call(f32[256,128]{1,0:T(8,128)S(1)} %bitcast.3, f32[4,128]{1,0:T(4,128)S(1)} %copy-done.1, s32[4,128]{1,0:T(4,128)S(1)} %copy-done.2, s32[4,128]{1,0:T(4,128)S(1)} %copy-done.3), custom_call_target="tpu_custom_call" | custom-call | tf_op jit(solution)/shard_map/coupled_steps/pallas_call | solution.py:455
  33.2 0.7 %copy.6 = f32[8,8,4,128]{3,2,1,0:T(4,128)} copy(f32[8,8,4,128]{3,2,1,0:T(4,128)S(1)} %bitcast.2) | data formatting | bytes 262144
Async XLA Ops:
  0.0 0.9 %copy-start = (f32[8,8,4,128]{3,2,1,0:T(4,128)S(1)}, f32[8,8,4,128]{3,2,1,0:T(4,128)}, u32[]{:S(2)}) copy-start(f32[8,8,4,128]{3,2,1,0:T(4,128)} %param.4) | copy-start | bytes 393220
  0.9 0.7 %copy-start.1 = (f32[4,128]{1,0:T(4,128)S(1)}, f32[4,128]{1,0:T(4,128)}, u32[]{:S(2)}) copy-start(f32[4,128]{1,0:T(4,128)} %irr.1) | copy-start | bytes 6148
  1.6 0.7 %copy-start.2 = (s32[4,128]{1,0:T(4,128)S(1)}, s32[4,128]{1,0:T(4,128)}, u32[]{:S(2)}) copy-start(s32[4,128]{1,0:T(4,128)} %land.1) | copy-start | bytes 6148
  2.3 0.7 %copy-start.3 = (s32[4,128]{1,0:T(4,128)S(1)}, s32[4,128]{1,0:T(4,128)}, u32[]{:S(2)}) copy-start(s32[4,128]{1,0:T(4,128)} %bottom.1) | copy-start | bytes 6148

commit v2 on v1

--- a/solution.py
+++ b/solution.py
@@ -195,20 +195,19 @@
 def kernel(
     gy_size, gx_size, state, irr, land, bottom, out,
     raw, irr_v, land_v, bottom_v, mine, other, packs, strips_in, strip, edges, strip_o, edges_o,
-    wet, press, next_d, next_t, nstrip, nedges,
-    load_sem, send_sem, recv_sem,
+    wet, press, next_d, next_t, nedges,
+    load_sem, send_sem, recv_sem, hello_west, hello_north,
 ):
     comp, gy, gx = (lax.axis_index(a) for a in ("comp", "gy", "gx"))
     east, west = lax.rem(gx + 1, gx_size), lax.rem(gx + gx_size - 1, gx_size)
     up, down = lax.rem(gy + 1, gy_size), lax.rem(gy + gy_size - 1, gy_size)
     twin = 1 - comp
-    places = [(up, east), (up, west), (down, east), (down, west), (up, gx), (down, gx), (gy, east), (gy, west)]
+    eastern = [(c, y, east) for y in (up, gy, down) for c in (comp, twin)]
+    western = [(c, y, west) for y in (up, gy, down) for c in (comp, twin)]
 
     barrier = pltpu.get_barrier_semaphore()
-    for y, x in places:
-        for c in (comp, twin):
-            pl.semaphore_signal(barrier, inc=1, device_id=(c, y, x), device_id_type=MESH)
-    pl.semaphore_signal(barrier, inc=1, device_id=(twin, gy, gx), device_id_type=MESH)
+    for target in western + [(comp, up, gx), (twin, up, gx), (twin, gy, gx)]:
+        pl.semaphore_signal(barrier, inc=1, device_id=target, device_id_type=MESH)
 
     loads = [
         pltpu.make_async_copy(src, dst, load_sem.at[i])
@@ -236,7 +235,11 @@
     packs[0] = jnp.where(slot < 2, rows, lanes(lit_rows, 2))
     packs[1] = jnp.where(slot < 2, lanes(lit_rows, -2), rows)
 
-    pl.semaphore_wait(barrier, 2 * len(places) + 1)
+    pl.semaphore_wait(barrier, 9)
+    for target in eastern:
+        pl.semaphore_signal(hello_west, inc=1, device_id=target, device_id_type=MESH)
+    for target in [(comp, down, gx), (twin, down, gx)]:
+        pl.semaphore_signal(hello_north, inc=1, device_id=target, device_id_type=MESH)
 
     def remote(index, src, dst, target):
         return pltpu.make_async_remote_copy(
@@ -262,53 +265,66 @@
     flow_own = remote(16, mine.at[0:8, 2:6], other.at[0:8, 2:6], (twin, gy, gx))
     plant_own = remote(16, mine.at[0:5, 2:6], other.at[0:5, 2:6], (twin, gy, gx))
 
-    dyn_sends = same_rows[:4] + twin_rows[:4] + same_rows[4:] + twin_rows[4:] + same_cols + flow_cols + [flow_own]
-    trc_sends = same_rows + twin_rows[4:] + same_cols + plant_cols + [plant_own]
-
-    @pl.when(comp == 0)
-    def _():
-        for copy in dyn_sends:
+    dyn_west = [same_rows[0], same_rows[2], twin_rows[0], twin_rows[2], same_cols[0], flow_cols[0]]
+    dyn_east = [same_rows[1], same_rows[3], twin_rows[1], twin_rows[3], same_cols[1], flow_cols[1]]
+    trc_west = [same_rows[0], same_rows[2], same_cols[0], plant_cols[0]]
+    trc_east = [same_rows[1], same_rows[3], same_cols[1], plant_cols[1]]
+    to_north = [same_rows[4], twin_rows[4]]
+    to_south = [same_rows[5], twin_rows[5]]
+
+    def start(copies):
+        for copy in copies:
             copy.start()
 
-    @pl.when(comp == 1)
-    def _():
-        for copy in trc_sends:
-            copy.start()
+    def arrived(copies):
+        for copy in copies:
+            copy.wait_recv()
 
     no_south, no_north = gy == 0, gy == gy_size - 1
-    col3 = quad % 4 == 3
     low = lane < 64
     middle = (lane >= 32) & (lane < 96)
     inner = (lane % 64 >= 4) & (lane % 64 < 20)
 
-    def build(own_rows, arrived, fields, store):
-        south = jnp.where(slot < 2, arrived[SOUTH], own_rows)
-        north = lanes(jnp.where(slot < 2, own_rows, arrived[NORTH]), 64)
-        se, nw, ne = lanes(arrived[SE], 32), lanes(arrived[NW], 64), lanes(arrived[NE], 96)
+    def strip_rows(own_rows, south, north, fields, store):
+        south = jnp.where(slot < 2, south, own_rows)
+        north = lanes(jnp.where(slot < 2, own_rows, north), 64)
         halves = (jnp.where(low, south, north), jnp.where(low, north, south))
-        corners = (
-            jnp.where(col3, jnp.where(low, arrived[SW], nw), jnp.where(middle, se, ne)),
-            jnp.where(col3, jnp.where(low, nw, arrived[SW]), jnp.where(middle, ne, se)),
+        for f in fields:
+            store(f, jnp.where(inner, lanes(halves[f // 4], 4 - 16 * f), 0.0))
+
+    def strip_corners(south, north, is_east, fields, load, store):
+        south, north = (lanes(south, 32), lanes(north, 96)) if is_east else (south, lanes(north, 64))
+        first = middle if is_east else low
+        halves = (jnp.where(first, south, north), jnp.where(first, north, south))
+        there = lane % 64 // 4 == (5 if is_east else 0)
+        for f in fields:
+            store(f, jnp.where(there, lanes(halves[f // 4], -12 - 16 * f), load(f)))
+
+    def lit_side(s):
+        southern = s in (SOUTH, SW, SE)
+        return jnp.where(no_south if southern else no_north, 0.0, lanes(strips_in[0, s], -2 if southern else 2))
+
+    def keeper(ref, edge_ref, shift=0):
+        def store(f, value):
+            ref[f + shift] = value
+            edge_ref[f + shift] = row_edges(value)
+
+        return store
+
+    def start_strips(other_fields):
+        strip_rows(rows, strips_in[0, SOUTH], strips_in[0, NORTH], range(8), keeper(strip, edges))
+        strip_rows(lit_rows, lit_side(SOUTH), lit_side(NORTH), [0], keeper(strip, edges, 8))
+        strip_rows(
+            other_own_rows(other_fields), strips_in[1, SOUTH], strips_in[1, NORTH], other_fields, keeper(strip_o, edges_o)
         )
-        for f in fields:
-            store(f, jnp.where(inner, lanes(halves[f // 4], 4 - 16 * f), lanes(corners[f // 4], -12 - 16 * f)))
-
-    def strips(lit_sides, own_strip, own_edges, my_fields, other_rows, other_fields):
-        def keep(ref, edge_ref):
-            def store(f, value):
-                ref[f] = value
-                edge_ref[f] = row_edges(value)
-
-            return store
-
-        build(own_strip, [strips_in[0, s] for s in range(6)], my_fields, keep(strip, edges))
-        lit_in = []
-        for s in range(6):
-            southern = s in (SOUTH, SW, SE)
-            dry = no_south if southern else no_north
-            lit_in.append(jnp.where(dry, 0.0, lanes(strips_in[0, s], -2 if southern else 2)))
-        build(lit_sides, lit_in, [0], lambda f, value: keep(strip, edges)(8, value))
-        build(other_rows, [strips_in[1, s] for s in range(6)], other_fields, keep(strip_o, edges_o))
+
+    def add_corners(south, north, is_east, other_fields):
+        args = (strips_in[0, south], strips_in[0, north], is_east)
+        strip_corners(*args, range(8), lambda f: strip[f], keeper(strip, edges))
+        strip_corners(lit_side(south), lit_side(north), is_east, [0], lambda f: strip[8], keeper(strip, edges, 8))
+        if other_fields:
+            args = (strips_in[1, south], strips_in[1, north], is_east)
+            strip_corners(*args, other_fields, lambda f: strip_o[f], keeper(strip_o, edges_o))
 
     def other_own_rows(fields):
         result = jnp.zeros((LEV, LANES), jnp.float32)
@@ -317,13 +333,15 @@
                 result = jnp.where(quad == 4 * f + x, lanes(other[f, OWN + x], 16 * f + 4 * x + 2), result)
         return result
 
-    def wet_everywhere():
-        for col in range(8):
+    def wet_columns(cols):
+        for col in cols:
             wet[0, col] = (mine[8, col] > 0).astype(jnp.float32)
-        wet_strip = (strip[8] > 0).astype(jnp.float32)
-        wet_edges = row_edges(wet_strip)
-        at = {col: wet_faces(around(lambda c: wet[0, c], wet_edges, col)) for col in range(1, 7)}
-        return at, wet_faces(around_strip(wet_strip)), wet_strip
+
+    def wet_strip():
+        return (strip[8] > 0).astype(jnp.float32)
+
+    def wet_at(col):
+        return wet_faces(around(lambda c: wet[0, c], row_edges(wet_strip()), col))
 
     first_row = gy * LANES
     coriolis_main = 0.3 + 0.4 * (first_row + lane).astype(jnp.float32) / float(gy_size * LANES)
@@ -333,116 +351,152 @@
     def store_out(f, x, value):
         out[pl.ds(f * 32 + x, 8, stride=4), :] = value
 
-    @pl.when(comp == 0)
-    def _():
-        for copy in [flow_own] + plant_cols + same_cols + twin_rows[4:] + same_rows:
-            if copy is flow_own:
-                plant_own.wait_recv()
-            else:
-                copy.wait_recv()
-        strips(lit_rows, rows, None, range(8), other_own_rows((2, 3)), (2, 3))
-        wet_at, wet_h, wet_strip = wet_everywhere()
-        for col in range(8):
+    def full_step(now, before, p, wets, coriolis, heating):
+        u, v = step_speeds(now, before, p, wets, coriolis)
+        t, s = step_heat_salt(now, before, wets, heating)
+        after = jnp.stack([u, v, t, s])
+        return after, filtered(now[0], before[0], after, wets[0])
+
+    def tracer_step(c, u, v, wets, temp, salt, lit):
+        kappa = mixing_of(temp, salt, wets[0])
+        light = light_of(c[0][2], c[0][3], lit)
+        change = transported(c, u, v, wets) + mixed(c[0], kappa) + reactions(c[0], temp, light)
+        return c[0] + 0.1 * change * wets[0]
+
+    def dyn_pressure(cols):
+        for col in cols:
             press[0, col] = pressure_of(mine[2, col], mine[3, col], wet[0, col])
-        press_h = pressure_of(strip[2], strip[3], wet_strip)
-        press_e = row_edges(press_h)
-
-        def full_step(now, before, p, wets, coriolis, heating):
-            u, v = step_speeds(now, before, p, wets, coriolis)
-            t, s = step_heat_salt(now, before, wets, heating)
-            after = jnp.stack([u, v, t, s])
-            return after, filtered(now[0], before[0], after, wets[0])
-
-        h_now, h_before = around_strip(strip[0:4]), around_strip(strip[4:8])
-        h_heat = heating_of(strip_o[2], strip_o[3], strip[8], wet_strip)
-        after, filt = full_step(h_now, h_before, around_strip(press_h), wet_h, coriolis_strip, h_heat)
-        nstrip[0:4], nstrip[4:8] = after, filt
+
+    def dyn_strip():
+        dry = wet_strip()
+        p = around_strip(pressure_of(strip[2], strip[3], dry))
+        heat = heating_of(strip_o[2], strip_o[3], strip[8], dry)
+        now, before = around_strip(strip[0:4]), around_strip(strip[4:8])
+        after, filt = full_step(now, before, p, wet_faces(around_strip(dry)), coriolis_strip, heat)
         nedges[0:4], nedges[4:8] = row_edges(after), row_edges(filt)
-        for col in range(1, 7):
+        nedges[8] = row_edges(pressure_of(after[2], after[3], dry))
+
+    def dyn_first(cols):
+        press_e = row_edges(pressure_of(strip[2], strip[3], wet_strip()))
+        for col in cols:
+            wets = wet_at(col)
             now = around(lambda c: mine[0:4, c], edges[0:4], col)
             before = around(lambda c: mine[4:8, c], edges[4:8], col)
             p = around(lambda c: press[0, c], press_e, col)
-            heat = heating_of(other[2, col], other[3, col], mine[8, col], wet[0, col])
-            after, filt = full_step(now, before, p, wet_at[col], coriolis_main, heat)
+            heat = heating_of(other[2, col], other[3, col], mine[8, col], wets[0])
+            after, filt = full_step(now, before, p, wets, coriolis_main, heat)
             next_d[0:4, col], next_d[4:8, col] = after, filt
-        for col in range(2, 6):
-            c = other[0:5, col]
-            u = around(lambda c: mine[0, c], edges[0], col)
-            v = around(lambda c: mine[1, c], edges[1], col)
-            plants = around(lambda c: other[2:4, c], edges_o[2:4], col)
-            kappa = mixing_of(mine[2, col], mine[3, col], wet[0, col])
-            light = light_of(c[2], c[3], mine[8, col])
-            change = transported(plants, u[:3], (v[0], v[3], v[4]), wet_at[col]) + mixed(plants[0], kappa)
-            change = change + plant_reactions(c, mine[2, col], light)
-            next_t[2:4, col] = plants[0] + 0.1 * change * wet[0, col]
-        for col in range(1, 7):
-            press[1, col] = pressure_of(next_d[2, col], next_d[3, col], wet[0, col])
-        press_e = row_edges(pressure_of(nstrip[2], nstrip[3], wet_strip))
-        for col in range(2, 6):
+            press[1, col] = pressure_of(after[2], after[3], wets[0])
+            if 2 <= col < 6:
+                c = other[0:5, col]
+                plants = around(lambda c: other[2:4, c], edges_o[2:4], col)
+                u = (now[0][0], now[1][0], now[2][0])
+                v = (now[0][1], now[3][1], now[4][1])
+                kappa = mixing_of(now[0][2], now[0][3], wets[0])
+                light = light_of(c[2], c[3], mine[8, col])
+                change = transported(plants, u, v, wets) + mixed(plants[0], kappa)
+                change = change + plant_reactions(c, now[0][2], light)
+                next_t[2:4, col] = plants[0] + 0.1 * change * wets[0]
+
+    def dyn_second(cols):
+        for col in cols:
+            wets = wet_at(col)
             now = around(lambda c: next_d[0:4, c], nedges[0:4], col)
             before = around(lambda c: next_d[4:8, c], nedges[4:8], col)
-            p = around(lambda c: press[1, c], press_e, col)
-            heat = heating_of(next_t[2, col], next_t[3, col], mine[8, col], wet[0, col])
-            after, filt = full_step(now, before, p, wet_at[col], coriolis_main, heat)
+            p = around(lambda c: press[1, c], nedges[8], col)
+            heat = heating_of(next_t[2, col], next_t[3, col], mine[8, col], wets[0])
+            after, filt = full_step(now, before, p, wets, coriolis_main, heat)
             for f in range(4):
                 store_out(f, col - 2, after[f])
                 store_out(4 + f, col - 2, filt[f])
 
-    @pl.when(comp == 1)
-    def _():
-        for copy in [flow_own] + flow_cols + same_cols + twin_rows[4:] + same_rows[4:] + twin_rows[:4] + same_rows[:4]:
-            copy.wait_recv()
-        strips(lit_rows, rows, None, range(8), other_own_rows(range(8)), range(8))
-        wet_at, wet_h, wet_strip = wet_everywhere()
-        for col in range(8):
+    def trc_pressure(cols):
+        for col in cols:
             press[0, col] = pressure_of(other[2, col], other[3, col], wet[0, col])
-        press_h = pressure_of(strip_o[2], strip_o[3], wet_strip)
-        press_e = row_edges(press_h)
-
-        def tracer_step(c, u, v, wets, temp, salt, lit):
-            kappa = mixing_of(temp, salt, wets[0])
-            light = light_of(c[0][2], c[0][3], lit)
-            change = transported(c, u, v, wets) + mixed(c[0], kappa) + reactions(c[0], temp, light)
-            return c[0] + 0.1 * change * wets[0]
-
+
+    def trc_strip():
+        dry = wet_strip()
+        wets = wet_faces(around_strip(dry))
+        p = around_strip(pressure_of(strip_o[2], strip_o[3], dry))
         now, before = around_strip(strip_o[0:4]), around_strip(strip_o[4:6])
-        u, v = step_speeds(now, before, around_strip(press_h), wet_h, coriolis_strip)
+        u, v = step_speeds(now, before, p, wets, coriolis_strip)
         nedges[8], nedges[9] = row_edges(u), row_edges(v)
         u = (now[0][0], now[1][0], now[2][0])
         v = (now[0][1], now[3][1], now[4][1])
-        new = tracer_step(around_strip(strip[0:8]), u, v, wet_h, strip_o[2], strip_o[3], strip[8])
-        nedges[0:8] = row_edges(new)
-        for col in range(1, 7):
+        nedges[0:8] = row_edges(tracer_step(around_strip(strip[0:8]), u, v, wets, strip_o[2], strip_o[3], strip[8]))
+
+    def trc_first(cols):
+        press_e = row_edges(pressure_of(strip_o[2], strip_o[3], wet_strip()))
+        for col in cols:
+            wets = wet_at(col)
             now = around(lambda c: other[0:4, c], edges_o[0:4], col)
             before = around(lambda c: other[4:8, c], edges_o[4:8], col)
             p = around(lambda c: press[0, c], press_e, col)
-            next_d[0, col], next_d[1, col] = step_speeds(now, before, p, wet_at[col], coriolis_main)
+            next_d[0, col], next_d[1, col] = step_speeds(now, before, p, wets, coriolis_main)
             c = around(lambda c: mine[0:8, c], edges[0:8], col)
             if 2 <= col < 6:
-                heat = heating_of(c[0][2], c[0][3], mine[8, col], wet[0, col])
-                next_d[2, col], next_d[3, col] = step_heat_salt(now, before, wet_at[col], heat)
+                heat = heating_of(c[0][2], c[0][3], mine[8, col], wets[0])
+                next_d[2, col], next_d[3, col] = step_heat_salt(now, before, wets, heat)
             u = (now[0][0], now[1][0], now[2][0])
             v = (now[0][1], now[3][1], now[4][1])
-            next_t[0:8, col] = tracer_step(c, u, v, wet_at[col], other[2, col], other[3, col], mine[8, col])
-        for col in range(2, 6):
+            next_t[0:8, col] = tracer_step(c, u, v, wets, now[0][2], now[0][3], mine[8, col])
+
+    def trc_second(cols):
+        for col in cols:
             c = around(lambda c: next_t[0:8, c], nedges[0:8], col)
             u = around(lambda c: next_d[0, c], nedges[8], col)
             v = around(lambda c: next_d[1, c], nedges[9], col)
             new = tracer_step(
-                c, u[:3], (v[0], v[3], v[4]), wet_at[col], next_d[2, col], next_d[3, col], mine[8, col]
+                c, u[:3], (v[0], v[3], v[4]), wet_at(col), next_d[2, col], next_d[3, col], mine[8, col]
             )
             for f in range(8):
                 store_out(f, col - 2, new[f])
 
+    def run(own, own_in, west_out, east_out, west_in, east_in, rows_of, pressure, at_strip, first, second, corner_fields):
+        start(west_out + to_south + [own])
+        pl.semaphore_wait(hello_north, 2)
+        start(to_north)
+        arrived([own_in] + to_north + to_south)
+        start_strips(rows_of)
+        wet_columns(range(2, 6))
+        pressure(range(2, 6))
+        first((3, 4))
+        pl.semaphore_wait(hello_west, 6)
+        start(east_out)
+        arrived(east_in)
+        add_corners(SE, NE, True, corner_fields)
+        wet_columns((6, 7))
+        pressure((6, 7))
+        first((5, 6))
+        at_strip()
+        second((4, 5))
+        arrived(west_in)
+        add_corners(SW, NW, False, corner_fields)
+        wet_columns((0, 1))
+        pressure((0, 1))
+        first((1, 2))
+        at_strip()
+        second((2, 3))
+        for copy in [own] + west_out + east_out + to_north + to_south:
+            copy.wait_send()
+
     @pl.when(comp == 0)
     def _():
-        for copy in dyn_sends:
-            copy.wait_send()
+        run(
+            flow_own, plant_own, dyn_west, dyn_east,
+            [same_rows[0], same_rows[2], same_cols[0], plant_cols[0]],
+            [same_rows[1], same_rows[3], same_cols[1], plant_cols[1]],
+            (2, 3), dyn_pressure, dyn_strip, dyn_first, dyn_second, (),
+        )
 
     @pl.when(comp == 1)
     def _():
-        for copy in trc_sends:
-            copy.wait_send()
+        run(
+            plant_own, flow_own, trc_west, trc_east,
+            [same_rows[0], same_rows[2], twin_rows[0], twin_rows[2], same_cols[0], flow_cols[0]],
+            [same_rows[1], same_rows[3], twin_rows[1], twin_rows[3], same_cols[1], flow_cols[1]],
+            range(8), trc_pressure, trc_strip, trc_first, trc_second, range(8),
+        )
 
 
 def solution(mesh):
@@ -452,6 +506,7 @@
         rows = ocean_state.size // LANES
         anywhere = pl.BlockSpec(memory_space=pl.ANY)
         f32 = jnp.float32
+        operands = (ocean_state.reshape(rows, LANES), irradiance, land_mask, bottom_level)
         result = pl.pallas_call(
             functools.partial(kernel, gy_size, gx_size),
             out_shape=jax.ShapeDtypeStruct((rows, LANES), f32),
@@ -474,17 +529,18 @@
                 pltpu.VMEM((2, 8, LEV, LANES), f32),
                 pltpu.VMEM((8, 8, LEV, LANES), f32),
                 pltpu.VMEM((8, 8, LEV, LANES), f32),
-                pltpu.VMEM((8, LEV, LANES), f32),
                 pltpu.VMEM((10, LEV, LANES), f32),
                 pltpu.SemaphoreType.DMA((4,)),
                 pltpu.SemaphoreType.DMA((17,)),
                 pltpu.SemaphoreType.DMA((17,)),
+                pltpu.SemaphoreType.REGULAR,
+                pltpu.SemaphoreType.REGULAR,
             ],
             compiler_params=pltpu.CompilerParams(
                 collective_id=0, has_side_effects=True, vmem_limit_bytes=8 * 1024 * 1024
             ),
             name="coupled_steps",
-        )(ocean_state.reshape(rows, LANES), irradiance, land_mask, bottom_level)
+        )(*[pltpu.with_memory_space_constraint(a, pltpu.HBM) for a in operands])
         return result.reshape(ocean_state.shape)
 
     return jax.shard_map(

time: 34.1 us -> 29.4 us (0.86)
  local copies, waits for them, and re-layouts: 3.6 us -> 0.66 us
  Pallas kernels: 30.3 us -> 28.6 us
    unnamed x9 -> x1, local copies, waits for them, and re-layouts: 3.6 us -> 0.66 us
    pallas_call x1, Pallas kernels: 30.3 us -> 28.6 us  [local(): pl.pallas_call(functools.partial(kernel, gy_size, gx_size), out_shape=jax...]
where the time goes in v2:
time: 29.4 us; the launch traced here: 29.2 us
  Pallas kernels  28.6 us (97%)
  local copies, waits for them, and re-layouts  0.66 us (2%)
    pallas_call x1, Pallas kernels, local(): pl.pallas_call(functools.partial(kernel, gy_size, gx_size), out_shape=jax...  28.6 us
    unnamed x1, local copies, waits for them, and re-layouts  0.66 us

profile of v2, /device:TPU:1, one launch (start us, length us, event | category | flops | bytes accessed | tf_op | source)
XLA Modules:
  0.0 29.2 jit_solution(5400328095768963284)
XLA Ops:
  0.0 28.6 %coupled_steps.1 = f32[256,128]{1,0:T(8,128)S(1)} custom-call(f32[256,128]{1,0:T(8,128)} %bitcast.3, f32[4,128]{1,0:T(4,128)} %irr.1, s32[4,128]{1,0:T(4,128)} %land.1, s32[4,128]{1,0:T(4,128)} %bottom.1), custom_call_target="tpu_custom_call" | custom-call | tf_op jit(solution)/shard_map/coupled_steps/pallas_call | solution.py:510
  28.6 0.7 %copy.6 = f32[8,8,4,128]{3,2,1,0:T(4,128)} copy(f32[8,8,4,128]{3,2,1,0:T(4,128)S(1)} %bitcast.2) | data formatting | bytes 262144

commit v3 on v2

v3 whole, which is shorter than its diff:
```python
import functools

import jax
import jax.numpy as jnp
from jax import lax
from jax.experimental import pallas as pl
from jax.experimental.pallas import tpu as pltpu
from jax.sharding import PartitionSpec as P

MESH = pl.DeviceIdType.MESH

SW, SE, NW, NE = range(4)
OWN = 2
LEV, LANES = 8, 128


def roll(value, shift, axis):
    return pltpu.roll(value, shift % value.shape[axis] if isinstance(shift, int) else shift, axis)


def lanes(value, shift):
    return roll(value, shift, value.ndim - 1)


def levels(value, shift):
    return roll(value, shift, value.ndim - 2)


def iota(dim):
    return lax.broadcasted_iota(jnp.int32, (LEV, LANES), dim)


def level_sum(value):
    k = iota(0)
    for shift in (1, 2, 4):
        value = value + jnp.where(k >= shift, levels(value, shift), 0.0)
    return value


def density(temp, salt, wet):
    return (0.8 * salt - 0.2 * temp) * wet


def pressure_of(temp, salt, wet):
    return 0.1 * level_sum(density(temp, salt, wet))


def mixing_of(temp, salt, wet):
    rho = density(temp, salt, wet)
    strat = jnp.maximum(levels(rho, -1) - rho, 0.0)
    wet_below = jnp.where(iota(0) == LEV - 1, 0.0, levels(wet, -1))
    return (0.05 + 1.0 / (1.0 + 4.0 * strat)) * wet * wet_below


def absorbed(small, large):
    absorb = 0.08 + 0.05 * (jnp.abs(small) + jnp.abs(large))
    return absorb, level_sum(absorb)


def surface_of(lit):
    return jnp.broadcast_to(lit[0:1, :], (LEV, LANES))


def heating_of(small, large, lit, wet):
    absorb, column = absorbed(small, large)
    return surface_of(lit) * (jnp.exp(absorb - column) - jnp.exp(-column)) * wet


def light_of(small, large, lit):
    absorb, column = absorbed(small, large)
    return surface_of(lit) * jnp.exp(0.5 * absorb - column)


def gradients(p, wet):
    pc, pe, pw, pn, ps = p
    _, we, ww, wn, ws = wet
    return 0.5 * (we * (pe - pc) + ww * (pc - pw)), 0.5 * (wn * (pn - pc) + ws * (pc - ps))


def spread_of(field, wet):
    c, e, w, n, s = field
    _, we, ww, wn, ws = wet
    return we * (e - c) + ww * (w - c) + wn * (n - c) + ws * (s - c)


def faces(u, v, wet):
    (uc, ue, uw), (vc, vn, vs) = u, v
    _, we, ww, wn, ws = wet
    return 0.25 * (uc + ue) * we, 0.25 * (uc + uw) * ww, 0.25 * (vc + vn) * wn, 0.25 * (vc + vs) * ws


def carried_of(field, face):
    c, e, w, n, s = field
    fe, fw, fn, fs = face
    return fe * (c + e) - fw * (c + w) + fn * (c + n) - fs * (c + s)


def pick(five, index):
    return tuple(part[index] for part in five)


def step_speeds(now, before, p, wet, coriolis):
    force_east, force_north = gradients(p, wet)
    u, v = now[0][0], now[0][1]
    du = coriolis * v - force_east + 0.2 * spread_of(pick(before, 0), wet)
    dv = -coriolis * u - force_north + 0.2 * spread_of(pick(before, 1), wet)
    return before[0][0] + 0.2 * du * wet[0], before[0][1] + 0.2 * dv * wet[0]


def step_heat_salt(now, before, wet, heating):
    u = (now[0][0], now[1][0], now[2][0])
    v = (now[0][1], now[3][1], now[4][1])
    face = faces(u, v, wet)
    dt = -carried_of(pick(now, 2), face) + 0.2 * spread_of(pick(before, 2), wet) + 3.0 * heating
    ds = -carried_of(pick(now, 3), face) + 0.2 * spread_of(pick(before, 3), wet)
    return before[0][2] + 0.2 * dt * wet[0], before[0][3] + 0.2 * ds * wet[0]


def filtered(now, before, after, wet):
    return now + 0.1 * (before - 2.0 * now + after) * wet


def transported(field, u, v, wet):
    c, e, w, n, s = field
    _, we, ww, wn, ws = wet
    fe, fw, fn, fs = faces(u, v, wet)
    le, lw, ln, ls = 0.2 * we, 0.2 * ww, 0.2 * wn, 0.2 * ws
    own = (le + fe) + (lw - fw) + (ln + fn) + (ls - fs)
    return (le - fe) * e + (lw + fw) * w + (ln - fn) * n + (ls + fs) * s - own * c


def mixed(c, kappa):
    down = kappa * (levels(c, -1) - c)
    return down - levels(down, 1)


def growth_of(nitrate, ammonium, small, large, temp, light):
    rate = jnp.exp(0.06 * temp) * (light / (light + 0.5))
    both = jnp.abs(nitrate) + jnp.abs(ammonium)
    return 0.6 * rate * small / (0.2 + both), 0.9 * rate * large / (0.8 + both)


def reactions(c, temp, light):
    nn, na = jnp.abs(c[0]), jnp.abs(c[1])
    small, large = growth_of(c[0], c[1], c[2], c[3], temp, light)
    sn, sa, ln, la = small * nn, small * na, large * nn, large * na
    graze = 0.8 * c[4] / (1.0 + jnp.abs(c[2]) + jnp.abs(c[3]))
    gs, gl = graze * c[2], graze * c[3]
    remin = 0.3 * c[5] + 0.1 * c[6]
    nitrify = 0.2 * c[1]
    return jnp.stack(
        [
            nitrify - sn - ln,
            remin + 0.1 * c[4] - nitrify - sa - la,
            sn + sa - gs - 0.1 * c[2],
            ln + la - gl - 0.1 * c[3],
            0.7 * (gs + gl) - 0.1 * c[4] - 0.15 * c[4],
            0.1 * c[2] + 0.3 * gs - 0.3 * c[5],
            0.1 * c[3] + 0.15 * c[4] + 0.3 * gl - 0.1 * c[6],
            1.3 * (sn + sa + ln + la) - (remin + 2.0 * nitrify),
        ]
    )


def plant_reactions(c, temp, light):
    both = jnp.abs(c[0]) + jnp.abs(c[1])
    small, large = growth_of(c[0], c[1], c[2], c[3], temp, light)
    graze = 0.8 * c[4] / (1.0 + jnp.abs(c[2]) + jnp.abs(c[3]))
    return jnp.stack([small * both - graze * c[2] - 0.1 * c[2], large * both - graze * c[3] - 0.1 * c[3]])


def row_edges(strip):
    slot = iota(1) % 4
    return jnp.where(slot == 2, lanes(strip, 64), strip)


def around(columns, edges, col):
    lane = iota(1)
    c = columns(col)
    edge = lanes(edges, LANES - 2 - 4 * (col - 1))
    north = lanes(jnp.where(lane == 0, edge, c), -1)
    south = lanes(jnp.where(lane == LANES - 1, edge, c), 1)
    return c, columns(col + 1), columns(col - 1), north, south


def around_strip(strip):
    return strip, lanes(strip, -4), lanes(strip, 4), lanes(strip, -1), lanes(strip, 1)


def wet_faces(wet):
    c, e, w, n, s = wet
    return c, c * e, c * w, c * n, c * s


def speeds_of(now):
    return (now[0][0], now[1][0], now[2][0]), (now[0][1], now[3][1], now[4][1])


def kernel(
    gy_size, gx_size, state, irr, land, bottom, out,
    raw, irr_v, land_v, bottom_v, mine, other, packs, pairs, corners_in, rows_in, strip, edges, strip_o, edges_o,
    wet, press, next_d, next_t, nedges,
    load_sem, send_sem, recv_sem, hello, intro,
):
    comp, gy, gx = (lax.axis_index(a) for a in ("comp", "gy", "gx"))
    east, west = lax.rem(gx + 1, gx_size), lax.rem(gx + gx_size - 1, gx_size)
    up, down = lax.rem(gy + 1, gy_size), lax.rem(gy + gy_size - 1, gy_size)
    twin = 1 - comp
    eastern = [(c, y, east) for y in (up, down, gy) for c in (comp, twin)]
    western = [(c, y, west) for y in (up, down, gy) for c in (comp, twin)]

    barrier = pltpu.get_barrier_semaphore()
    for target in western + [(twin, gy, gx)]:
        pl.semaphore_signal(barrier, inc=1, device_id=target, device_id_type=MESH)

    loads = [
        pltpu.make_async_copy(src, dst, load_sem.at[i])
        for i, (src, dst) in enumerate([(irr, irr_v), (land, land_v), (bottom, bottom_v), (state, raw)])
    ]
    for load in loads:
        load.start()

    pl.semaphore_wait(barrier, 7)
    for target in eastern:
        pl.semaphore_signal(hello, inc=1, device_id=target, device_id_type=MESH)
    for load in loads:
        load.wait()

    lane, k = iota(1), iota(0)
    slot, quad = lane % 4, lane // 4
    blank = jnp.zeros((LEV, LANES), jnp.float32)

    def take(x, carry):
        rows, lit_rows = carry
        is_wet = (land_v[pl.ds(x, 1), :] == 1) & (k < bottom_v[pl.ds(x, 1), :])
        lit = jnp.where(is_wet, jnp.broadcast_to(irr_v[pl.ds(x, 1), :], (LEV, LANES)), 0.0)
        mine[8, OWN + x] = lit
        lit_rows = jnp.where(quad == x, lanes(lit, 4 * x + 2), lit_rows)
        for f in range(8):
            value = raw[pl.ds(f * 32 + x, 8, stride=4), :]
            mine[f, OWN + x] = value
            rows = jnp.where(quad == 4 * f + x, lanes(value, lax.rem(16 * f + 4 * x + 2, LANES)), rows)
        return rows, lit_rows

    rows, lit_rows = lax.fori_loop(0, 4, take, (blank, blank))
    packs[0] = jnp.where(slot < 2, rows, lanes(lit_rows, 2))
    packs[1] = jnp.where(slot < 2, lanes(lit_rows, -2), rows)

    def remote(index, src, dst, target):
        return pltpu.make_async_remote_copy(
            src_ref=src, dst_ref=dst, send_sem=send_sem.at[index], recv_sem=recv_sem.at[index],
            device_id=target, device_id_type=MESH,
        )

    ways = [(SW, 0, up, east), (SE, 0, up, west), (NW, 1, down, east), (NE, 1, down, west)]
    same_corners = [remote(s, packs.at[p], corners_in.at[0, s], (comp, y, x)) for s, p, y, x in ways]
    twin_corners = [remote(4 + s, packs.at[p], corners_in.at[1, s], (twin, y, x)) for s, p, y, x in ways]
    row_sends = [
        remote(8 + 2 * p + c, pairs.at[p], rows_in.at[p], (c, y, gx)) for p, y in ((0, up), (1, down)) for c in (0, 1)
    ]
    same_cols = [
        remote(12, mine.at[:, 4:6], mine.at[:, 0:2], (comp, gy, east)),
        remote(13, mine.at[:, 2:4], mine.at[:, 6:8], (comp, gy, west)),
    ]
    flow_cols = [
        remote(14, mine.at[0:8, 4:6], other.at[0:8, 0:2], (twin, gy, east)),
        remote(15, mine.at[0:8, 2:4], other.at[0:8, 6:8], (twin, gy, west)),
    ]
    plant_cols = [
        remote(14, mine.at[2:4, 5:6], other.at[2:4, 1:2], (twin, gy, east)),
        remote(15, mine.at[2:4, 2:3], other.at[2:4, 6:7], (twin, gy, west)),
    ]
    flow_own = remote(16, mine.at[0:8, 2:6], other.at[0:8, 2:6], (twin, gy, gx))
    plant_own = remote(16, mine.at[0:5, 2:6], other.at[0:5, 2:6], (twin, gy, gx))
    pack_own = remote(17, packs, pairs.at[:, 1], (twin, gy, gx))

    dyn_east = [same_corners[SW], twin_corners[SW], same_corners[NW], twin_corners[NW], same_cols[0], flow_cols[0]]
    dyn_west = [same_corners[SE], twin_corners[SE], same_corners[NE], twin_corners[NE], same_cols[1], flow_cols[1]]
    trc_east = [same_corners[SW], same_corners[NW], same_cols[0], plant_cols[0]]
    trc_west = [same_corners[SE], same_corners[NE], same_cols[1], plant_cols[1]]

    def start(copies):
        for copy in copies:
            copy.start()

    def arrived(copies):
        for copy in copies:
            copy.wait_recv()

    def sent(copies):
        for copy in copies:
            copy.wait_send()

    no_south, no_north = gy == 0, gy == gy_size - 1
    low = lane < 64
    inner = (lane % 64 >= 4) & (lane % 64 < 20)

    def keep(ref, edge_ref, f, value):
        ref[f] = value
        edge_ref[f] = row_edges(value)

    def lit_part(value, southern):
        return jnp.where(no_south if southern else no_north, 0.0, lanes(value, -2 if southern else 2))

    def other_rows_of(fields):
        def add(x, result):
            for f in fields:
                value = lanes(other[f, OWN + x], lax.rem(16 * f + 4 * x + 2, LANES))
                result = jnp.where(quad == 4 * f + x, value, result)
            return result

        return lax.fori_loop(0, 4, add, blank)

    def start_strips(me, plants_only):
        def halves_of(own_rows, south, north):
            south = jnp.where(slot < 2, south, own_rows)
            north = lanes(jnp.where(slot < 2, own_rows, north), 64)
            return jnp.where(low, south, north), jnp.where(low, north, south)

        def put(ref, edge_ref, f, half, by=None):
            keep(ref, edge_ref, f, jnp.where(inner, lanes(half, 4 - 16 * f if by is None else by), 0.0))

        south, north = rows_in[0, me], rows_in[1, me]
        south_o, north_o = rows_in[0, 1 - me], rows_in[1, 1 - me]
        first, last = halves_of(rows, south, north)
        lit_first, _ = halves_of(lit_rows, lit_part(south, True), lit_part(north, False))
        put(strip, edges, 8, lit_first, 4)
        first_o, last_o = halves_of(other_rows_of((2, 3) if plants_only else range(8)), south_o, north_o)

        def field(f, carry):
            by, by_last = lax.rem(LANES + 4 - 16 * f, LANES), 68 - 16 * f
            put(strip, edges, f, first, by)
            put(strip, edges, f + 4, last, by_last)
            if not plants_only:
                put(strip_o, edges_o, f, first_o, by)
                put(strip_o, edges_o, f + 4, last_o, by_last)
            return carry

        lax.fori_loop(0, 4, field, 0)
        if plants_only:
            for f in (2, 3):
                put(strip_o, edges_o, f, first_o)

    def add_corners(is_east, plants_only):
        left = 32 * is_east
        there = lane % 64 // 4 == 5 * is_east
        first = (lane >= left) & (lane < 64 + left)

        def halves_of(south, north):
            south, north = lanes(south, left), lanes(north, 64 + left)
            return jnp.where(first, south, north), jnp.where(first, north, south)

        def put(ref, edge_ref, f, half, by):
            keep(ref, edge_ref, f, jnp.where(there, lanes(half, by), ref[f]))

        south, north = corners_in[0, is_east], corners_in[0, 2 + is_east]
        lit_half, _ = halves_of(lit_part(south, True), lit_part(north, False))
        put(strip, edges, 8, lit_half, LANES - 12)
        first_half, last_half = halves_of(south, north)
        if not plants_only:
            first_o, last_o = halves_of(corners_in[1, is_east], corners_in[1, 2 + is_east])

        def field(f, carry):
            by, by_last = LANES - 12 - 16 * f, lax.rem(2 * LANES - 76 - 16 * f, LANES)
            put(strip, edges, f, first_half, by)
            put(strip, edges, f + 4, last_half, by_last)
            if not plants_only:
                put(strip_o, edges_o, f, first_o, by)
                put(strip_o, edges_o, f + 4, last_o, by_last)
            return carry

        lax.fori_loop(0, 4, field, 0)

    def wet_strip():
        return (strip[8] > 0).astype(jnp.float32)

    def wet_at(col, wet_edges):
        return wet_faces(around(lambda c: wet[0, c], wet_edges, col))

    first_row = gy * LANES
    coriolis_main = 0.3 + 0.4 * (first_row + lane).astype(jnp.float32) / float(gy_size * LANES)
    strip_row = first_row + slot + jnp.where(low, -2, LANES - 2)
    coriolis_strip = 0.3 + 0.4 * strip_row.astype(jnp.float32) / float(gy_size * LANES)

    def store_out(f, col, value):
        out[pl.ds(f * 32 + col - OWN, 8, stride=4), :] = value

    def full_step(now, before, p, wets, coriolis, heating):
        u, v = step_speeds(now, before, p, wets, coriolis)
        t, s = step_heat_salt(now, before, wets, heating)
        after = jnp.stack([u, v, t, s])
        return after, filtered(now[0], before[0], after, wets[0])

    def tracer_step(c, u, v, wets, temp, salt, lit):
        kappa = mixing_of(temp, salt, wets[0])
        light = light_of(c[0][2], c[0][3], lit)
        change = transported(c, u, v, wets) + mixed(c[0], kappa) + reactions(c[0], temp, light)
        return c[0] + 0.1 * change * wets[0]

    def dyn_strip():
        dry = wet_strip()
        p = around_strip(pressure_of(strip[2], strip[3], dry))
        heat = heating_of(strip_o[2], strip_o[3], strip[8], dry)
        now, before = around_strip(strip[0:4]), around_strip(strip[4:8])
        after, filt = full_step(now, before, p, wet_faces(around_strip(dry)), coriolis_strip, heat)
        nedges[0:4], nedges[4:8] = row_edges(after), row_edges(filt)
        nedges[8] = row_edges(pressure_of(after[2], after[3], dry))

    def dyn_first(col, wet_edges, press_edges):
        wets = wet_at(col, wet_edges)
        now = around(lambda c: mine[0:4, c], edges[0:4], col)
        before = around(lambda c: mine[4:8, c], edges[4:8], col)
        p = around(lambda c: press[0, c], press_edges, col)
        heat = heating_of(other[2, col], other[3, col], mine[8, col], wets[0])
        after, filt = full_step(now, before, p, wets, coriolis_main, heat)
        next_d[0:4, col], next_d[4:8, col] = after, filt
        press[1, col] = pressure_of(after[2], after[3], wets[0])

        @pl.when((col >= OWN) & (col < OWN + 4))
        def _():
            c = other[0:5, col]
            plants = around(lambda c: other[2:4, c], edges_o[2:4], col)
            kappa = mixing_of(now[0][2], now[0][3], wets[0])
            light = light_of(c[2], c[3], mine[8, col])
            change = transported(plants, *speeds_of(now), wets) + mixed(plants[0], kappa)
            change = change + plant_reactions(c, now[0][2], light)
            next_t[2:4, col] = plants[0] + 0.1 * change * wets[0]

    def dyn_second(col, wet_edges):
        wets = wet_at(col, wet_edges)
        now = around(lambda c: next_d[0:4, c], nedges[0:4], col)
        before = around(lambda c: next_d[4:8, c], nedges[4:8], col)
        p = around(lambda c: press[1, c], nedges[8], col)
        heat = heating_of(next_t[2, col], next_t[3, col], mine[8, col], wets[0])
        after, filt = full_step(now, before, p, wets, coriolis_main, heat)
        for f in range(4):
            store_out(f, col, after[f])
            store_out(4 + f, col, filt[f])

    def trc_strip():
        dry = wet_strip()
        wets = wet_faces(around_strip(dry))
        p = around_strip(pressure_of(strip_o[2], strip_o[3], dry))
        now, before = around_strip(strip_o[0:4]), around_strip(strip_o[4:6])
        u, v = step_speeds(now, before, p, wets, coriolis_strip)
        nedges[8], nedges[9] = row_edges(u), row_edges(v)
        c = around_strip(strip[0:8])
        nedges[0:8] = row_edges(tracer_step(c, *speeds_of(now), wets, strip_o[2], strip_o[3], strip[8]))

    def trc_first(col, wet_edges, press_edges):
        wets = wet_at(col, wet_edges)
        now = around(lambda c: other[0:4, c], edges_o[0:4], col)
        before = around(lambda c: other[4:8, c], edges_o[4:8], col)
        p = around(lambda c: press[0, c], press_edges, col)
        next_d[0, col], next_d[1, col] = step_speeds(now, before, p, wets, coriolis_main)
        c = around(lambda c: mine[0:8, c], edges[0:8], col)
        heat = heating_of(c[0][2], c[0][3], mine[8, col], wets[0])
        next_d[2, col], next_d[3, col] = step_heat_salt(now, before, wets, heat)
        next_t[0:8, col] = tracer_step(c, *speeds_of(now), wets, now[0][2], now[0][3], mine[8, col])

    def trc_second(col, wet_edges):
        c = around(lambda c: next_t[0:8, c], nedges[0:8], col)
        u = around(lambda c: next_d[0, c], nedges[8], col)
        v = around(lambda c: next_d[1, c], nedges[9], col)
        new = tracer_step(
            c, u[:3], (v[0], v[3], v[4]), wet_at(col, wet_edges), next_d[2, col], next_d[3, col], mine[8, col]
        )
        for f in range(8):
            store_out(f, col, new[f])

    def phases(me, own_in, at_east, east_in, west_in, flow, flow_strip, first, at_strip, second):
        def phase(it, carry):
            @pl.when(it == 0)
            def _():
                arrived([own_in, row_sends[me], row_sends[2 + me]])
                start_strips(me, me == 0)

            @pl.when(it == 1)
            def _():
                at_east()
                arrived(east_in)

            @pl.when(it == 2)
            def _():
                arrived(west_in)

            @pl.when(it > 0)
            def _():
                add_corners(2 - it, me == 0)

            dry = wet_strip()
            wet_edges = row_edges(dry)
            press_edges = row_edges(pressure_of(flow_strip[2], flow_strip[3], dry))

            def ready(col, carry):
                is_wet = (mine[8, col] > 0).astype(jnp.float32)
                wet[0, col] = is_wet
                press[0, col] = pressure_of(flow[2, col], flow[3, col], is_wet)
                return carry

            def one(col, carry):
                first(col, wet_edges, press_edges)
                return carry

            def two(col, carry):
                second(col, wet_edges)
                return carry

            begin = jnp.where(it == 0, 2, jnp.where(it == 1, 6, 0))
            lax.fori_loop(begin, begin + jnp.where(it == 0, 4, 2), ready, 0)
            begin = jnp.where(it == 0, 3, jnp.where(it == 1, 5, 1))
            lax.fori_loop(begin, begin + 2, one, 0)

            @pl.when(it > 0)
            def _():
                at_strip()
                lax.fori_loop(6 - 2 * it, 8 - 2 * it, two, 0)

            return carry

        lax.fori_loop(0, 3, phase, 0)

    @pl.when(comp == 0)
    def _():
        start(dyn_east + [flow_own])
        pairs[0, 0] = packs[0]
        pairs[1, 0] = packs[1]
        arrived([pack_own])
        pl.semaphore_wait(intro, 1)
        start(row_sends)

        def at_east():
            pl.semaphore_wait(hello, 6)
            start(dyn_west)

        east_in = [same_corners[SE], same_corners[NE], same_cols[1], plant_cols[1]]
        west_in = [same_corners[SW], same_corners[NW], same_cols[0], plant_cols[0]]
        phases(0, plant_own, at_east, east_in, west_in, mine, strip, dyn_first, dyn_strip, dyn_second)
        sent(dyn_east + [flow_own] + row_sends + dyn_west)

    @pl.when(comp == 1)
    def _():
        start([pack_own] + trc_east + [plant_own])
        pl.semaphore_wait(hello, 6)
        pl.semaphore_signal(intro, inc=1, device_id=(twin, gy, west), device_id_type=MESH)
        start(trc_west)
        east_in = [same_corners[SE], same_corners[NE], twin_corners[SE], twin_corners[NE], same_cols[1], flow_cols[1]]
        west_in = [same_corners[SW], same_corners[NW], twin_corners[SW], twin_corners[NW], same_cols[0], flow_cols[0]]
        phases(1, flow_own, lambda: None, east_in, west_in, other, strip_o, trc_first, trc_strip, trc_second)
        sent([pack_own] + trc_east + [plant_own] + trc_west)


def solution(mesh):
    gy_size, gx_size = mesh.shape["gy"], mesh.shape["gx"]

    def local(ocean_state, irradiance, land_mask, bottom_level):
        rows = ocean_state.size // LANES
        anywhere = pl.BlockSpec(memory_space=pl.ANY)
        f32 = jnp.float32
        operands = (ocean_state.reshape(rows, LANES), irradiance, land_mask, bottom_level)
        result = pl.pallas_call(
            functools.partial(kernel, gy_size, gx_size),
            out_shape=jax.ShapeDtypeStruct((rows, LANES), f32),
            in_specs=[anywhere] * 4,
            out_specs=pl.BlockSpec(memory_space=pltpu.VMEM),
            scratch_shapes=[
                pltpu.VMEM((rows, LANES), f32),
                pltpu.VMEM((4, LANES), f32),
                pltpu.VMEM((4, LANES), jnp.int32),
                pltpu.VMEM((4, LANES), jnp.int32),
                pltpu.VMEM((9, 8, LEV, LANES), f32),
                pltpu.VMEM((8, 8, LEV, LANES), f32),
                pltpu.VMEM((2, LEV, LANES), f32),
                pltpu.VMEM((2, 2, LEV, LANES), f32),
                pltpu.VMEM((2, 4, LEV, LANES), f32),
                pltpu.VMEM((2, 2, LEV, LANES), f32),
                pltpu.VMEM((9, LEV, LANES), f32),
                pltpu.VMEM((9, LEV, LANES), f32),
                pltpu.VMEM((8, LEV, LANES), f32),
                pltpu.VMEM((8, LEV, LANES), f32),
                pltpu.VMEM((1, 8, LEV, LANES), f32),
                pltpu.VMEM((2, 8, LEV, LANES), f32),
                pltpu.VMEM((8, 8, LEV, LANES), f32),
                pltpu.VMEM((8, 8, LEV, LANES), f32),
                pltpu.VMEM((10, LEV, LANES), f32),
                pltpu.SemaphoreType.DMA((4,)),
                pltpu.SemaphoreType.DMA((18,)),
                pltpu.SemaphoreType.DMA((18,)),
                pltpu.SemaphoreType.REGULAR,
                pltpu.SemaphoreType.REGULAR,
            ],
            compiler_params=pltpu.CompilerParams(
                collective_id=0, has_side_effects=True, vmem_limit_bytes=8 * 1024 * 1024
            ),
            name="coupled_steps",
        )(*[pltpu.with_memory_space_constraint(a, pltpu.HBM) for a in operands])
        return result.reshape(ocean_state.shape)

    return jax.shard_map(
        local,
        mesh=mesh,
        in_specs=(P("comp", None, "gx", "gy"), P("gx", "gy"), P("gx", "gy"), P("gx", "gy")),
        out_specs=P("comp", None, "gx", "gy"),
        check_vma=False,
    )
```

time: 29.4 us -> 30.5 us (1.037); the launches traced: 29.2 us -> 30 us
  Pallas kernels: 28.6 us -> 29.3 us
    pallas_call x1, Pallas kernels: 28.6 us -> 29.3 us  [local(): pl.pallas_call(functools.partial(kernel, gy_size, gx_size), out_shape=jax...]
where the time goes in v3:
time: 30.5 us; the launch traced here: 30 us
  Pallas kernels  29.3 us (96%)
  local copies, waits for them, and re-layouts  0.66 us (2%)
    pallas_call x1, Pallas kernels, local(): pl.pallas_call(functools.partial(kernel, gy_size, gx_size), out_shape=jax...  29.3 us
    unnamed x1, local copies, waits for them, and re-layouts  0.66 us

profile of v3, /device:TPU:1, one launch (start us, length us, event | category | flops | bytes accessed | tf_op | source)
XLA Modules:
  0.0 30.0 jit_solution(5542551305215388883)
XLA Ops:
  0.0 29.3 %coupled_steps.1 = f32[256,128]{1,0:T(8,128)S(1)} custom-call(f32[256,128]{1,0:T(8,128)} %bitcast.3, f32[4,128]{1,0:T(4,128)} %irr.1, s32[4,128]{1,0:T(4,128)} %land.1, s32[4,128]{1,0:T(4,128)} %bottom.1), custom_call_target="tpu_custom_call" | custom-call | tf_op jit(solution)/shard_map/coupled_steps/pallas_call | solution.py:561
  29.3 0.7 %copy.6 = f32[8,8,4,128]{3,2,1,0:T(4,128)} copy(f32[8,8,4,128]{3,2,1,0:T(4,128)S(1)} %bitcast.2) | data formatting | bytes 262144

commit v4 on v3

--- a/solution.py
+++ b/solution.py
@@ -230,21 +230,11 @@
     slot, quad = lane % 4, lane // 4
     blank = jnp.zeros((LEV, LANES), jnp.float32)
 
-    def take(x, carry):
-        rows, lit_rows = carry
-        is_wet = (land_v[pl.ds(x, 1), :] == 1) & (k < bottom_v[pl.ds(x, 1), :])
-        lit = jnp.where(is_wet, jnp.broadcast_to(irr_v[pl.ds(x, 1), :], (LEV, LANES)), 0.0)
-        mine[8, OWN + x] = lit
-        lit_rows = jnp.where(quad == x, lanes(lit, 4 * x + 2), lit_rows)
+    for x in (2, 3, 0, 1):
+        is_wet = (land_v[x : x + 1, :] == 1) & (k < bottom_v[x : x + 1, :])
+        mine[8, OWN + x] = jnp.where(is_wet, jnp.broadcast_to(irr_v[x : x + 1, :], (LEV, LANES)), 0.0)
         for f in range(8):
-            value = raw[pl.ds(f * 32 + x, 8, stride=4), :]
-            mine[f, OWN + x] = value
-            rows = jnp.where(quad == 4 * f + x, lanes(value, lax.rem(16 * f + 4 * x + 2, LANES)), rows)
-        return rows, lit_rows
-
-    rows, lit_rows = lax.fori_loop(0, 4, take, (blank, blank))
-    packs[0] = jnp.where(slot < 2, rows, lanes(lit_rows, 2))
-    packs[1] = jnp.where(slot < 2, lanes(lit_rows, -2), rows)
+            mine[f, OWN + x] = raw[pl.ds(f * 32 + x, 8, stride=4), :]
 
     def remote(index, src, dst, target):
         return pltpu.make_async_remote_copy(
@@ -291,6 +281,22 @@
         for copy in copies:
             copy.wait_send()
 
+    @pl.when(comp == 0)
+    def _():
+        start([same_cols[0], flow_cols[0]])
+
+    @pl.when(comp == 1)
+    def _():
+        start([same_cols[0], plant_cols[0]])
+
+    rows, lit_rows = blank, blank
+    for x in range(4):
+        for f in range(8):
+            rows = jnp.where(quad == 4 * f + x, lanes(mine[f, OWN + x], 16 * f + 4 * x + 2), rows)
+        lit_rows = jnp.where(quad == x, lanes(mine[8, OWN + x], 4 * x + 2), lit_rows)
+    packs[0] = jnp.where(slot < 2, rows, lanes(lit_rows, 2))
+    packs[1] = jnp.where(slot < 2, lanes(lit_rows, -2), rows)
+
     no_south, no_north = gy == 0, gy == gy_size - 1
     low = lane < 64
     inner = (lane % 64 >= 4) & (lane % 64 < 20)
@@ -303,13 +309,11 @@
         return jnp.where(no_south if southern else no_north, 0.0, lanes(value, -2 if southern else 2))
 
     def other_rows_of(fields):
-        def add(x, result):
+        result = blank
+        for x in range(4):
             for f in fields:
-                value = lanes(other[f, OWN + x], lax.rem(16 * f + 4 * x + 2, LANES))
-                result = jnp.where(quad == 4 * f + x, value, result)
-            return result
-
-        return lax.fori_loop(0, 4, add, blank)
+                result = jnp.where(quad == 4 * f + x, lanes(other[f, OWN + x], 16 * f + 4 * x + 2), result)
+        return result
 
     def start_strips(me, plants_only):
         def halves_of(own_rows, south, north):
@@ -317,29 +321,21 @@
             north = lanes(jnp.where(slot < 2, own_rows, north), 64)
             return jnp.where(low, south, north), jnp.where(low, north, south)
 
-        def put(ref, edge_ref, f, half, by=None):
-            keep(ref, edge_ref, f, jnp.where(inner, lanes(half, 4 - 16 * f if by is None else by), 0.0))
+        def put(ref, edge_ref, f, half, by):
+            keep(ref, edge_ref, f, jnp.where(inner, lanes(half, by), 0.0))
 
         south, north = rows_in[0, me], rows_in[1, me]
         south_o, north_o = rows_in[0, 1 - me], rows_in[1, 1 - me]
         first, last = halves_of(rows, south, north)
         lit_first, _ = halves_of(lit_rows, lit_part(south, True), lit_part(north, False))
         put(strip, edges, 8, lit_first, 4)
-        first_o, last_o = halves_of(other_rows_of((2, 3) if plants_only else range(8)), south_o, north_o)
-
-        def field(f, carry):
-            by, by_last = lax.rem(LANES + 4 - 16 * f, LANES), 68 - 16 * f
-            put(strip, edges, f, first, by)
-            put(strip, edges, f + 4, last, by_last)
-            if not plants_only:
-                put(strip_o, edges_o, f, first_o, by)
-                put(strip_o, edges_o, f + 4, last_o, by_last)
-            return carry
-
-        lax.fori_loop(0, 4, field, 0)
-        if plants_only:
-            for f in (2, 3):
-                put(strip_o, edges_o, f, first_o)
+        fields = (2, 3) if plants_only else range(8)
+        halves = (first, last)
+        halves_o = halves_of(other_rows_of(fields), south_o, north_o)
+        for f in range(8):
+            put(strip, edges, f, halves[f // 4], 4 - 16 * f)
+        for f in fields:
+            put(strip_o, edges_o, f, halves_o[f // 4], 4 - 16 * f)
 
     def add_corners(is_east, plants_only):
         left = 32 * is_east
@@ -355,21 +351,14 @@
 
         south, north = corners_in[0, is_east], corners_in[0, 2 + is_east]
         lit_half, _ = halves_of(lit_part(south, True), lit_part(north, False))
-        put(strip, edges, 8, lit_half, LANES - 12)
-        first_half, last_half = halves_of(south, north)
+        put(strip, edges, 8, lit_half, -12)
+        halves = halves_of(south, north)
+        for f in range(8):
+            put(strip, edges, f, halves[f // 4], -12 - 16 * f)
         if not plants_only:
-            first_o, last_o = halves_of(corners_in[1, is_east], corners_in[1, 2 + is_east])
-
-        def field(f, carry):
-            by, by_last = LANES - 12 - 16 * f, lax.rem(2 * LANES - 76 - 16 * f, LANES)
-            put(strip, edges, f, first_half, by)
-            put(strip, edges, f + 4, last_half, by_last)
-            if not plants_only:
-                put(strip_o, edges_o, f, first_o, by)
-                put(strip_o, edges_o, f + 4, last_o, by_last)
-            return carry
-
-        lax.fori_loop(0, 4, field, 0)
+            halves_o = halves_of(corners_in[1, is_east], corners_in[1, 2 + is_east])
+            for f in range(8):
+                put(strip_o, edges_o, f, halves_o[f // 4], -12 - 16 * f)
 
     def wet_strip():
         return (strip[8] > 0).astype(jnp.float32)
@@ -416,8 +405,7 @@
         next_d[0:4, col], next_d[4:8, col] = after, filt
         press[1, col] = pressure_of(after[2], after[3], wets[0])
 
-        @pl.when((col >= OWN) & (col < OWN + 4))
-        def _():
+        if OWN <= col < OWN + 4:
             c = other[0:5, col]
             plants = around(lambda c: other[2:4, c], edges_o[2:4], col)
             kappa = mixing_of(now[0][2], now[0][3], wets[0])
@@ -454,8 +442,9 @@
         p = around(lambda c: press[0, c], press_edges, col)
         next_d[0, col], next_d[1, col] = step_speeds(now, before, p, wets, coriolis_main)
         c = around(lambda c: mine[0:8, c], edges[0:8], col)
-        heat = heating_of(c[0][2], c[0][3], mine[8, col], wets[0])
-        next_d[2, col], next_d[3, col] = step_heat_salt(now, before, wets, heat)
+        if OWN <= col < OWN + 4:
+            heat = heating_of(c[0][2], c[0][3], mine[8, col], wets[0])
+            next_d[2, col], next_d[3, col] = step_heat_salt(now, before, wets, heat)
         next_t[0:8, col] = tracer_step(c, *speeds_of(now), wets, now[0][2], now[0][3], mine[8, col])
 
     def trc_second(col, wet_edges):
@@ -468,85 +457,52 @@
         for f in range(8):
             store_out(f, col, new[f])
 
-    def phases(me, own_in, at_east, east_in, west_in, flow, flow_strip, first, at_strip, second):
-        def phase(it, carry):
-            @pl.when(it == 0)
-            def _():
-                arrived([own_in, row_sends[me], row_sends[2 + me]])
+    def phases(me, own_in, east_in, west_in, flow, flow_strip, first, at_strip, second):
+        inputs = [own_in, row_sends[me], row_sends[2 + me]], east_in, west_in
+        for it, (new, todo) in enumerate([(range(2, 6), (3, 4)), ((6, 7), (5, 6)), ((0, 1), (2, 1))]):
+            arrived(inputs[it])
+            if it == 0:
                 start_strips(me, me == 0)
-
-            @pl.when(it == 1)
-            def _():
-                at_east()
-                arrived(east_in)
-
-            @pl.when(it == 2)
-            def _():
-                arrived(west_in)
-
-            @pl.when(it > 0)
-            def _():
+            else:
                 add_corners(2 - it, me == 0)
-
             dry = wet_strip()
             wet_edges = row_edges(dry)
             press_edges = row_edges(pressure_of(flow_strip[2], flow_strip[3], dry))
-
-            def ready(col, carry):
+            for col in new:
                 is_wet = (mine[8, col] > 0).astype(jnp.float32)
                 wet[0, col] = is_wet
                 press[0, col] = pressure_of(flow[2, col], flow[3, col], is_wet)
-                return carry
-
-            def one(col, carry):
+            for col in todo:
                 first(col, wet_edges, press_edges)
-                return carry
-
-            def two(col, carry):
-                second(col, wet_edges)
-                return carry
-
-            begin = jnp.where(it == 0, 2, jnp.where(it == 1, 6, 0))
-            lax.fori_loop(begin, begin + jnp.where(it == 0, 4, 2), ready, 0)
-            begin = jnp.where(it == 0, 3, jnp.where(it == 1, 5, 1))
-            lax.fori_loop(begin, begin + 2, one, 0)
-
-            @pl.when(it > 0)
-            def _():
+            if it > 0:
                 at_strip()
-                lax.fori_loop(6 - 2 * it, 8 - 2 * it, two, 0)
-
-            return carry
-
-        lax.fori_loop(0, 3, phase, 0)
+                for col in (6 - 2 * it, 7 - 2 * it):
+                    second(col, wet_edges)
 
     @pl.when(comp == 0)
     def _():
-        start(dyn_east + [flow_own])
+        start(dyn_east[:4] + [flow_own])
         pairs[0, 0] = packs[0]
         pairs[1, 0] = packs[1]
         arrived([pack_own])
         pl.semaphore_wait(intro, 1)
         start(row_sends)
-
-        def at_east():
-            pl.semaphore_wait(hello, 6)
-            start(dyn_west)
-
+        pl.semaphore_wait(hello, 6)
+        start(dyn_west)
         east_in = [same_corners[SE], same_corners[NE], same_cols[1], plant_cols[1]]
         west_in = [same_corners[SW], same_corners[NW], same_cols[0], plant_cols[0]]
-        phases(0, plant_own, at_east, east_in, west_in, mine, strip, dyn_first, dyn_strip, dyn_second)
+        phases(0, plant_own, east_in, west_in, mine, strip, dyn_first, dyn_strip, dyn_second)
         sent(dyn_east + [flow_own] + row_sends + dyn_west)
 
     @pl.when(comp == 1)
     def _():
-        start([pack_own] + trc_east + [plant_own])
+        start(trc_east[:2] + [pack_own, plant_own])
         pl.semaphore_wait(hello, 6)
         pl.semaphore_signal(intro, inc=1, device_id=(twin, gy, west), device_id_type=MESH)
         start(trc_west)
         east_in = [same_corners[SE], same_corners[NE], twin_corners[SE], twin_corners[NE], same_cols[1], flow_cols[1]]
         west_in = [same_corners[SW], same_corners[NW], twin_corners[SW], twin_corners[NW], same_cols[0], flow_cols[0]]
-        phases(1, flow_own, lambda: None, east_in, west_in, other, strip_o, trc_first, trc_strip, trc_second)
+        phases(1, flow_own, east_in, west_in, other, strip_o, trc_first, trc_strip, trc_second)
         sent([pack_own] + trc_east + [plant_own] + trc_west)
 
 

time: 30.5 us -> 29.4 us (0.964); the launches traced: 30 us -> 29.2 us
  Pallas kernels: 29.3 us -> 28.5 us
    pallas_call x1, Pallas kernels: 29.3 us -> 28.5 us  [local(): pl.pallas_call(functools.partial(kernel, gy_size, gx_size), out_shape=jax...]
where the time goes in v4:
time: 29.4 us; the launch traced here: 29.2 us
  Pallas kernels  28.5 us (97%)
  local copies, waits for them, and re-layouts  0.66 us (2%)
    pallas_call x1, Pallas kernels, local(): pl.pallas_call(functools.partial(kernel, gy_size, gx_size), out_shape=jax...  28.5 us
    unnamed x1, local copies, waits for them, and re-layouts  0.66 us

profile of v4, /device:TPU:1, one launch (start us, length us, event | category | flops | bytes accessed | tf_op | source)
XLA Modules:
  0.0 29.2 jit_solution(7201789572717228241)
XLA Ops:
  0.0 28.5 %coupled_steps.1 = f32[256,128]{1,0:T(8,128)S(1)} custom-call(f32[256,128]{1,0:T(8,128)} %bitcast.3, f32[4,128]{1,0:T(4,128)} %irr.1, s32[4,128]{1,0:T(4,128)} %land.1, s32[4,128]{1,0:T(4,128)} %bottom.1), custom_call_target="tpu_custom_call" | custom-call | tf_op jit(solution)/shard_map/coupled_steps/pallas_call | solution.py:517
  28.5 0.7 %copy.6 = f32[8,8,4,128]{3,2,1,0:T(4,128)} copy(f32[8,8,4,128]{3,2,1,0:T(4,128)S(1)} %bitcast.2) | data formatting | bytes 262144

commit v5 on v4

--- a/solution.py
+++ b/solution.py
@@ -209,9 +209,16 @@
     eastern = [(c, y, east) for y in (up, down, gy) for c in (comp, twin)]
     western = [(c, y, west) for y in (up, down, gy) for c in (comp, twin)]
 
+    run = gx_size // 2
+    last, foremost = lax.rem(gx, run) == run - 1, lax.rem(gx, run) == 0
+
     barrier = pltpu.get_barrier_semaphore()
     for target in western + [(twin, gy, gx)]:
         pl.semaphore_signal(barrier, inc=1, device_id=target, device_id_type=MESH)
+
+    @pl.when(jnp.logical_not(last))
+    def _():
+        pl.semaphore_signal(barrier, inc=1, device_id=(0, up, gx), device_id_type=MESH)
 
     loads = [
         pltpu.make_async_copy(src, dst, load_sem.at[i])
@@ -220,7 +227,13 @@
     for load in loads:
         load.start()
 
-    pl.semaphore_wait(barrier, 7)
+    by_barrier = jnp.logical_and(comp == 0, jnp.logical_not(last))
+    pl.semaphore_wait(barrier, jnp.where(by_barrier, 9, 7))
+
+    @pl.when(by_barrier)
+    def _():
+        pl.semaphore_signal(intro, inc=1, device_id=(0, down, gx), device_id_type=MESH)
+
     for target in eastern:
         pl.semaphore_signal(hello, inc=1, device_id=target, device_id_type=MESH)
     for load in loads:
@@ -498,7 +511,11 @@
     def _():
         start(trc_east[:2] + [pack_own, plant_own])
         pl.semaphore_wait(hello, 6)
-        pl.semaphore_signal(intro, inc=1, device_id=(twin, gy, west), device_id_type=MESH)
+
+        @pl.when(foremost)
+        def _():
+            pl.semaphore_signal(intro, inc=1, device_id=(0, gy, west), device_id_type=MESH)
+
         start(trc_west)
         east_in = [same_corners[SE], same_corners[NE], twin_corners[SE], twin_corners[NE], same_cols[1], flow_cols[1]]
         west_in = [same_corners[SW], same_corners[NW], twin_corners[SW], twin_corners[NW], same_cols[0], flow_cols[0]]

time: 29.4 us -> 29.4 us (level)
  no operation moved by 1% of the time
where the time goes in v5:
time: 29.4 us; the launch traced here: 29.2 us
  Pallas kernels  28.5 us (97%)
  local copies, waits for them, and re-layouts  0.66 us (2%)
    pallas_call x1, Pallas kernels, local(): pl.pallas_call(functools.partial(kernel, gy_size, gx_size), out_shape=jax...  28.5 us
    unnamed x1, local copies, waits for them, and re-layouts  0.66 us

profile of v5, /device:TPU:1, one launch (start us, length us, event | category | flops | bytes accessed | tf_op | source)
XLA Modules:
  0.0 29.2 jit_solution(18136114535495847838)
XLA Ops:
  0.0 28.5 %coupled_steps.1 = f32[256,128]{1,0:T(8,128)S(1)} custom-call(f32[256,128]{1,0:T(8,128)} %bitcast.3, f32[4,128]{1,0:T(4,128)} %irr.1, s32[4,128]{1,0:T(4,128)} %land.1, s32[4,128]{1,0:T(4,128)} %bottom.1), custom_call_target="tpu_custom_call" | custom-call | tf_op jit(solution)/shard_map/coupled_steps/pallas_call | solution.py:534
  28.6 0.7 %copy.6 = f32[8,8,4,128]{3,2,1,0:T(4,128)} copy(f32[8,8,4,128]{3,2,1,0:T(4,128)S(1)} %bitcast.2) | data formatting | bytes 262144

commit v6 on v5

--- a/solution.py
+++ b/solution.py
@@ -196,6 +196,20 @@
     return (now[0][0], now[1][0], now[2][0]), (now[0][1], now[3][1], now[4][1])
 
 
+class Guarded:
+    def __init__(self, copy, sends, receives):
+        self.copy, self.sends, self.receives = copy, sends, receives
+
+    def start(self):
+        pl.when(self.sends)(self.copy.start)
+
+    def wait_send(self):
+        pl.when(self.sends)(self.copy.wait_send)
+
+    def wait_recv(self):
+        pl.when(self.receives)(self.copy.wait_recv)
+
+
 def kernel(
     gy_size, gx_size, state, irr, land, bottom, out,
     raw, irr_v, land_v, bottom_v, mine, other, packs, pairs, corners_in, rows_in, strip, edges, strip_o, edges_o,
@@ -256,8 +270,23 @@
         )
 
     ways = [(SW, 0, up, east), (SE, 0, up, west), (NW, 1, down, east), (NE, 1, down, west)]
-    same_corners = [remote(s, packs.at[p], corners_in.at[0, s], (comp, y, x)) for s, p, y, x in ways]
-    twin_corners = [remote(4 + s, packs.at[p], corners_in.at[1, s], (twin, y, x)) for s, p, y, x in ways]
+    no_south, no_north = gy == 0, gy == gy_size - 1
+    inside = [(gy < gy_size - 1, gy > 0), (gy > 0, gy < gy_size - 1)]
+    same_corners = [
+        Guarded(remote(s, packs.at[p], corners_in.at[0, s], (comp, y, x)), *inside[p]) for s, p, y, x in ways
+    ]
+    twin_corners = [
+        Guarded(remote(4 + s, packs.at[p], corners_in.at[1, s], (twin, y, x)), *inside[p]) for s, p, y, x in ways
+    ]
+
+    @pl.when(no_south)
+    def _():
+        corners_in[:, SW : SE + 1] = jnp.zeros((2, 2, LEV, LANES), jnp.float32)
+
+    @pl.when(no_north)
+    def _():
+        corners_in[:, NW : NE + 1] = jnp.zeros((2, 2, LEV, LANES), jnp.float32)
+
     row_sends = [
         remote(8 + 2 * p + c, pairs.at[p], rows_in.at[p], (c, y, gx)) for p, y in ((0, up), (1, down)) for c in (0, 1)
     ]
@@ -310,7 +339,6 @@
     packs[0] = jnp.where(slot < 2, rows, lanes(lit_rows, 2))
     packs[1] = jnp.where(slot < 2, lanes(lit_rows, -2), rows)
 
-    no_south, no_north = gy == 0, gy == gy_size - 1
     low = lane < 64
     inner = (lane % 64 >= 4) & (lane % 64 < 20)
 

time: 29.4 us -> 27 us (0.918)
  Pallas kernels: 28.5 us -> 26.2 us
    pallas_call x1, Pallas kernels: 28.5 us -> 26.2 us  [local(): pl.pallas_call(functools.partial(kernel, gy_size, gx_size), out_shape=jax...]
where the time goes in v6:
time: 27 us; the launch traced here: 26.8 us
  Pallas kernels  26.2 us (97%)
  local copies, waits for them, and re-layouts  0.66 us (2%)
    pallas_call x1, Pallas kernels, local(): pl.pallas_call(functools.partial(kernel, gy_size, gx_size), out_shape=jax...  26.2 us
    unnamed x1, local copies, waits for them, and re-layouts  0.66 us

profile of v6, /device:TPU:1, one launch (start us, length us, event | category | flops | bytes accessed | tf_op | source)
XLA Modules:
  0.0 26.8 jit_solution(15104588657748524372)
XLA Ops:
  0.0 26.2 %coupled_steps.1 = f32[256,128]{1,0:T(8,128)S(1)} custom-call(f32[256,128]{1,0:T(8,128)} %bitcast.3, f32[4,128]{1,0:T(4,128)} %irr.1, s32[4,128]{1,0:T(4,128)} %land.1, s32[4,128]{1,0:T(4,128)} %bottom.1), custom_call_target="tpu_custom_call" | custom-call | tf_op jit(solution)/shard_map/coupled_steps/pallas_call | solution.py:562
  26.2 0.7 %copy.6 = f32[8,8,4,128]{3,2,1,0:T(4,128)} copy(f32[8,8,4,128]{3,2,1,0:T(4,128)S(1)} %bitcast.2) | data formatting | bytes 262144

commit v7 on v6

--- a/solution.py
+++ b/solution.py
@@ -223,6 +223,13 @@
     eastern = [(c, y, east) for y in (up, down, gy) for c in (comp, twin)]
     western = [(c, y, west) for y in (up, down, gy) for c in (comp, twin)]
 
+    loads = [
+        pltpu.make_async_copy(src, dst, load_sem.at[i])
+        for i, (src, dst) in enumerate([(state, raw), (irr, irr_v), (land, land_v), (bottom, bottom_v)])
+    ]
+    for load in loads:
+        load.start()
+
     run = gx_size // 2
     last, foremost = lax.rem(gx, run) == run - 1, lax.rem(gx, run) == 0
 
@@ -234,13 +241,6 @@
     def _():
         pl.semaphore_signal(barrier, inc=1, device_id=(0, up, gx), device_id_type=MESH)
 
-    loads = [
-        pltpu.make_async_copy(src, dst, load_sem.at[i])
-        for i, (src, dst) in enumerate([(irr, irr_v), (land, land_v), (bottom, bottom_v), (state, raw)])
-    ]
-    for load in loads:
-        load.start()
-
     by_barrier = jnp.logical_and(comp == 0, jnp.logical_not(last))
     pl.semaphore_wait(barrier, jnp.where(by_barrier, 9, 7))
 
@@ -248,8 +248,8 @@
     def _():
         pl.semaphore_signal(intro, inc=1, device_id=(0, down, gx), device_id_type=MESH)
 
-    for target in eastern:
-        pl.semaphore_signal(hello, inc=1, device_id=target, device_id_type=MESH)
+    for place, target in zip((1, 1, 0, 0, 2, 2), eastern):
+        pl.semaphore_signal(hello.at[place], inc=1, device_id=target, device_id_type=MESH)
     for load in loads:
         load.wait()
 
@@ -325,7 +325,7 @@
 
     @pl.when(comp == 0)
     def _():
-        start([same_cols[0], flow_cols[0]])
+        start([flow_cols[0], same_cols[0]])
 
     @pl.when(comp == 1)
     def _():
@@ -528,8 +528,11 @@
         arrived([pack_own])
         pl.semaphore_wait(intro, 1)
         start(row_sends)
-        pl.semaphore_wait(hello, 6)
-        start(dyn_west)
+        pl.semaphore_wait(hello.at[2], 2)
+        start([flow_cols[1], same_cols[1]])
+        pl.semaphore_wait(hello.at[0], 2)
+        pl.semaphore_wait(hello.at[1], 2)
+        start(dyn_west[:4])
         east_in = [same_corners[SE], same_corners[NE], same_cols[1], plant_cols[1]]
         west_in = [same_corners[SW], same_corners[NW], same_cols[0], plant_cols[0]]
         phases(0, plant_own, east_in, west_in, mine, strip, dyn_first, dyn_strip, dyn_second)
@@ -538,13 +541,16 @@
     @pl.when(comp == 1)
     def _():
         start(trc_east[:2] + [pack_own, plant_own])
-        pl.semaphore_wait(hello, 6)
+        pl.semaphore_wait(hello.at[2], 2)
+        start(trc_west[2:])
+        pl.semaphore_wait(hello.at[0], 2)
+        pl.semaphore_wait(hello.at[1], 2)
+        start(trc_west[:2])
 
         @pl.when(foremost)
         def _():
             pl.semaphore_signal(intro, inc=1, device_id=(0, gy, west), device_id_type=MESH)
 
-        start(trc_west)
         east_in = [same_corners[SE], same_corners[NE], twin_corners[SE], twin_corners[NE], same_cols[1], flow_cols[1]]
         west_in = [same_corners[SW], same_corners[NW], twin_corners[SW], twin_corners[NW], same_cols[0], flow_cols[0]]
         phases(1, flow_own, east_in, west_in, other, strip_o, trc_first, trc_strip, trc_second)
@@ -587,7 +593,7 @@
                 pltpu.SemaphoreType.DMA((4,)),
                 pltpu.SemaphoreType.DMA((18,)),
                 pltpu.SemaphoreType.DMA((18,)),
-                pltpu.SemaphoreType.REGULAR,
+                pltpu.SemaphoreType.REGULAR((3,)),
                 pltpu.SemaphoreType.REGULAR,
             ],
             compiler_params=pltpu.CompilerParams(

time: 27 us -> 26.9 us (level)
  no operation moved by 1% of the time
where the time goes in v7:
time: 26.9 us; the launch traced here: 26.7 us
  Pallas kernels  26.1 us (97%)
  local copies, waits for them, and re-layouts  0.66 us (2%)
    pallas_call x1, Pallas kernels, local(): pl.pallas_call(functools.partial(kernel, gy_size, gx_size), out_shape=jax...  26.1 us
    unnamed x1, local copies, waits for them, and re-layouts  0.66 us

profile of v7, /device:TPU:1, one launch (start us, length us, event | category | flops | bytes accessed | tf_op | source)
XLA Modules:
  0.0 26.7 jit_solution(514452809132910028)
XLA Ops:
  0.0 26.1 %coupled_steps.1 = f32[256,128]{1,0:T(8,128)S(1)} custom-call(f32[256,128]{1,0:T(8,128)} %bitcast.3, f32[4,128]{1,0:T(4,128)} %irr.1, s32[4,128]{1,0:T(4,128)} %land.1, s32[4,128]{1,0:T(4,128)} %bottom.1), custom_call_target="tpu_custom_call" | custom-call | tf_op jit(solution)/shard_map/coupled_steps/pallas_call | solution.py:568
  26.1 0.7 %copy.6 = f32[8,8,4,128]{3,2,1,0:T(4,128)} copy(f32[8,8,4,128]{3,2,1,0:T(4,128)S(1)} %bitcast.2) | data formatting | bytes 262144

commit v8 on v7

--- a/solution.py
+++ b/solution.py
@@ -329,7 +329,7 @@
 
     @pl.when(comp == 1)
     def _():
-        start([same_cols[0], plant_cols[0]])
+        start([plant_cols[0], same_cols[0]])
 
     rows, lit_rows = blank, blank
     for x in range(4):

time: 26.9 us -> 26.9 us (level)
  no operation moved by 1% of the time
where the time goes in v8:
time: 26.9 us; the launch traced here: 26.7 us
  Pallas kernels  26.1 us (97%)
  local copies, waits for them, and re-layouts  0.66 us (2%)
    pallas_call x1, Pallas kernels, local(): pl.pallas_call(functools.partial(kernel, gy_size, gx_size), out_shape=jax...  26.1 us
    unnamed x1, local copies, waits for them, and re-layouts  0.66 us

profile of v8, /device:TPU:1, one launch (start us, length us, event | category | flops | bytes accessed | tf_op | source)
XLA Modules:
  0.0 26.7 jit_solution(14640180021649091865)
XLA Ops:
  0.0 26.1 %coupled_steps.1 = f32[256,128]{1,0:T(8,128)S(1)} custom-call(f32[256,128]{1,0:T(8,128)} %bitcast.3, f32[4,128]{1,0:T(4,128)} %irr.1, s32[4,128]{1,0:T(4,128)} %land.1, s32[4,128]{1,0:T(4,128)} %bottom.1), custom_call_target="tpu_custom_call" | custom-call | tf_op jit(solution)/shard_map/coupled_steps/pallas_call | solution.py:568
  26.1 0.7 %copy.6 = f32[8,8,4,128]{3,2,1,0:T(4,128)} copy(f32[8,8,4,128]{3,2,1,0:T(4,128)S(1)} %bitcast.2) | data formatting | bytes 262144
